TPU v7x, 512 devices: a whole 4x8x8 slice. The times are simulated.
512 devices in a mesh: circ: 16 (over y_hi, x), sect: 32 (over z, y_lo, core).
Axes of the slice: x: 4, y: 8 (y_hi: 4, y_lo: 2; y = y_hi * 2 + y_lo), z: 8, core: 2. Of those that a mesh axis runs over, the one named last changes fastest.
Arguments:
- strain: bfloat16 [2048, 2, 36, 4096], P('circ', None, None, 'sect'), may hold values from -6 to 6
- region: int32 [36, 4096], P(None, 'sect'), may hold values from 0 to 7
- prior_peak: float32 [36, 4096], P(None, 'sect'), may hold values from 5 to 25
- temp_prev: float32 [36, 4096], P(None, 'sect'), may hold values from 0.5 to 1.5
- conductivity: float32 [36, 4096], P(None, 'sect'), may hold values from 0.5 to 2
- loss_moduli: float32 [8, 8], replicated, may hold values from 0.02 to 0.25
- mullins_loss: float32 [8], replicated, may hold values from 0.1 to 1
- stiffness: float32 [8], replicated, may hold values from 0.5 to 4
Outputs:
- temperature: float32 [36, 4096], P(None, 'sect')
- peak: float32 [36, 4096], P(None, 'sect')
- modulus: bfloat16 [2048, 36, 4096], P('circ', None, 'sect')
All inputs are finite; a program needn't handle non-finite values.
Results may differ from a plain program's by a relative error of at most 0.0023.
Values sent between devices are 32-bit elements; how exact they have to be, the bound alone decides.
No kernel may reach another device: no remote copies, remote signals or barrier semaphores. Data moves between devices by JAX's collectives and lax.ppermute only.
A program may use at most 64 MiB of HBM per device.

v0:
```python
import math

import jax
import jax.numpy as jnp
from jax import lax
from jax.sharding import PartitionSpec as P

COMP = 2
HARM = 8
SWEEPS = 4


sink_rate = 0.1


def extended_2(block, sides, width):
    for axis, dim in sides:
        count = lax.axis_size(axis)
        forward = [(i, i + 1) for i in range(count - 1)]
        backward = [(target, source) for source, target in forward]
        low = lax.ppermute(
            lax.slice_in_dim(block, block.shape[dim] - width, None, axis=dim), axis, forward
        )
        high = lax.ppermute(lax.slice_in_dim(block, 0, width, axis=dim), axis, backward)
        block = jnp.concatenate([low, block, high], axis=dim)
    return block


def hysteresis_heat(coeffs, region_flat, temp_flat, loss_moduli):
    harmonics = loss_moduli.shape[1]
    regions = loss_moduli.shape[0]
    onehot = (jnp.arange(regions, dtype=jnp.int32)[:, None] == region_flat[None, :]).astype(
        jnp.float32
    )
    loss_map = jnp.dot(loss_moduli.T, onehot, precision=lax.Precision.HIGHEST)
    power = jnp.sum(jnp.square(coeffs[:harmonics]) + jnp.square(coeffs[harmonics:]), axis=1)
    return jnp.exp(-0.5 * temp_flat) * jnp.sum(loss_map * power, axis=0)


def region_lookup(region, values):
    onehot = (jnp.arange(values.shape[0], dtype=jnp.int32)[:, None, None] == region[None]).astype(
        jnp.float32
    )
    return jnp.sum(onehot * values[:, None, None], axis=0)


def relax(extended, sources, conduct):
    padded = jnp.pad(extended, ((1, 1), (0, 0)))
    beside = padded[2:, 1:-1] + padded[:-2, 1:-1] + padded[1:-1, 2:] + padded[1:-1, :-2]
    return (sources + conduct * beside) / (4.0 * conduct + sink_rate)


def per_device(
    strain, region, prior_peak, temp_prev, conductivity, loss_moduli, mullins_loss, stiffness
):
    sec_dev = strain.shape[0]
    layers, columns = region.shape
    circ_count = lax.axis_size("circ")
    total_sections = sec_dev * circ_count
    first = lax.axis_index("circ") * sec_dev
    sections = first + jnp.arange(sec_dev, dtype=jnp.int32)
    orders = jnp.arange(1, HARM + 1, dtype=jnp.int32)
    phase = orders[:, None] * sections[None, :] % total_sections
    angle = phase.astype(jnp.float32) * (2.0 * math.pi / total_sections)
    table = jnp.concatenate([jnp.cos(angle), jnp.sin(angle)], 0).astype(jnp.bfloat16)
    partial_sums = jnp.dot(table, strain.reshape(sec_dev, -1), preferred_element_type=jnp.float32)
    partial_sums = partial_sums.reshape(2 * HARM, COMP, layers * columns)
    scale = 1.0 / jnp.sqrt(jnp.float32(total_sections))
    energy = jnp.sum(jnp.square(strain.astype(jnp.float32)), axis=1)
    top = lax.pmax(jnp.max(energy, axis=0), "circ")
    peak = jnp.maximum(prior_peak, top)
    region_flat = region.reshape(-1)
    temp_flat = temp_prev.reshape(-1)
    coeffs = lax.psum(partial_sums, "circ") * scale
    hysteresis = hysteresis_heat(coeffs, region_flat, temp_flat, loss_moduli)
    heat = hysteresis.reshape(layers, columns) + region_lookup(region, mullins_loss) * (
        peak - prior_peak
    )
    field = temp_prev
    for sweep_index in range(SWEEPS):
        extended = extended_2(field, (("sect", 1),), 1)
        field = relax(extended, heat, conductivity)
    factor = region_lookup(region, stiffness) * jnp.exp(-0.5 * field)
    modulus = (factor[None] * (1.0 - 0.5 * jnp.tanh((peak[None] - energy) / 4.0))).astype(
        jnp.bfloat16
    )
    return (field, peak, modulus)


def solution(mesh):
    placed = (
        P("circ", None, None, "sect"),
        P(None, "sect"),
        P(None, "sect"),
        P(None, "sect"),
        P(None, "sect"),
        P(),
        P(),
        P(),
    )
    return jax.shard_map(
        per_device,
        mesh=mesh,
        in_specs=placed,
        out_specs=(P(None, "sect"), P(None, "sect"), P("circ", None, "sect")),
        check_vma=False,
    )
```

profile of v0, /device:TPU:256, one launch (start us, length us, event | category | flops | bytes accessed | tf_op | source)
XLA Modules:
  0.0 234.3 jit_solution(4231406737891813828)
XLA Ops:
  7.2 0.0 copy-start
  7.2 0.0 all-reduce.6.cloned.1.call-start
  7.2 0.9 fusion.39
  8.1 2.0 collective-permute-start.1
  10.1 2.3 collective-permute-start
  12.5 5.9 %copy.14 = bf16[128,2,36,128]{0,3,2,1:T(8,128)(2,1)S(1)} copy(bf16[128,2,36,128]{3,1,2,0:T(2,128)(2,1)} %param.8) | data formatting | bytes 4718592 | tf_op args[0]
  18.4 0.1 cosine_convert_fusion
  18.5 1.5 fusion.30
  20.1 0.0 all-reduce.6.cloned.1.call-update
  20.1 0.0 copy-start.3
  20.1 0.0 copy-start.6
  20.1 0.0 copy-start.7
  20.1 0.0 copy-start.2
  20.1 7.9 %multiply_reduce_fusion = f32[128,36,128]{2,1,0:T(8,128)S(1)} fusion(bf16[128,2,36,128]{3,1,2,0:T(2,128)(2,1)} %param.8), kind=kLoop, calls=%fused_computation.2 | loop fusion | flops 2949120 | bytes 4718592 | tf_op jit(solution)/shard_map/reduce_sum | solution.py:69
  28.0 0.0 copy-start.1
  28.1 0.0 copy-start.5
  28.1 0.2 reduce_max.9
  28.3 0.0 copy-done.3
  28.3 0.0 copy-done.6
  28.3 0.0 copy-done.7
  28.3 0.2 select_reduce_fusion
  28.5 83.3 %pmax.7 = f32[36,128]{1,0:T(8,128)S(1)} all-reduce(f32[36,128]{1,0:T(8,128)S(1)} %reduce_max.9), channel_id=1, replica_groups=mesh['circ'=16,'sect'=32] {'circ'}, use_global_device_ids=true, to_apply=%region_6.7 | all-reduce | flops 4608 | bytes 36864 | tf_op jit(solution)/shard_map/pmax | solution.py:70
  111.7 0.0 collective-permute-done.1
  111.7 0.0 collective-permute-done
  111.7 0.0 copy-done.2
  111.7 0.1 select_maximum_fusion.6
  111.8 83.3 %all-reduce.6.cloned.1.call-done = f32[16,2,4608]{2,0,1:T(8,128)} async-done(((f32[16,2,4608]{2,0,1:T(8,128)}), f32[16,2,4608]{2,0,1:T(8,128)}) %all-reduce.6.cloned.1.call-update) | async-done | bytes 589840 | tf_op jit(solution)/shard_map/psum | solution.py:74
  195.2 1.1 broadcast_multiply_fusion
  196.3 0.0 copy-done
  196.3 0.3 fusion.1
  196.6 0.0 copy-done.1
  196.7 0.0 copy-done.5
  196.7 0.1 fusion.24
  196.8 0.0 copy-start.4
  196.8 0.1 fusion.38
  196.9 1.9 collective-permute-start.3
  198.8 2.4 %collective-permute-start.2 = (f32[36,1]{1,0:T(8,128)S(1)}, f32[36,1]{1,0:T(8,128)S(1)}, u32[]{:S(2)}, u32[]{:S(2)}) collective-permute-start(f32[36,1]{1,0:T(8,128)S(1)} %get-tuple-element.21), channel_id=1, source_target_pairs={{0,1},{1,2},{2,3},{3,4},{4,5},{5,6},{6,7},{7,8},{8,9},{9,10},{10,1... | collective-permute-start | bytes 440 | tf_op jit(solution)/shard_map/ppermute | solution.py:21
  201.2 0.0 collective-permute-done.3
  201.2 4.8 %collective-permute-done.2 = f32[36,1]{1,0:T(8,128)S(1)} collective-permute-done((f32[36,1]{1,0:T(8,128)S(1)}, f32[36,1]{1,0:T(8,128)S(1)}, u32[]{:S(2)}, u32[]{:S(2)}) %collective-permute-start.2) | collective-permute-done | bytes 176 | tf_op jit(solution)/shard_map/ppermute | solution.py:21
  206.0 0.1 select_maximum_fusion.4
  206.1 0.1 fusion.19
  206.2 0.1 fusion.37
  206.3 1.9 collective-permute-start.5
  208.2 2.4 %collective-permute-start.4 = (f32[36,1]{1,0:T(8,128)S(1)}, f32[36,1]{1,0:T(8,128)S(1)}, u32[]{:S(2)}, u32[]{:S(2)}) collective-permute-start(f32[36,1]{1,0:T(8,128)S(1)} %get-tuple-element.19), channel_id=1, source_target_pairs={{0,1},{1,2},{2,3},{3,4},{4,5},{5,6},{6,7},{7,8},{8,9},{9,10},{10,1... | collective-permute-start | bytes 440 | tf_op jit(solution)/shard_map/ppermute | solution.py:21
  210.6 0.0 collective-permute-done.5
  210.6 4.8 %collective-permute-done.4 = f32[36,1]{1,0:T(8,128)S(1)} collective-permute-done((f32[36,1]{1,0:T(8,128)S(1)}, f32[36,1]{1,0:T(8,128)S(1)}, u32[]{:S(2)}, u32[]{:S(2)}) %collective-permute-start.4) | collective-permute-done | bytes 176 | tf_op jit(solution)/shard_map/ppermute | solution.py:21
  215.4 0.1 select_maximum_fusion.2
  215.5 0.1 fusion.14
  215.6 0.1 fusion.36
  215.7 1.9 collective-permute-start.7
  217.6 2.4 %collective-permute-start.6 = (f32[36,1]{1,0:T(8,128)S(1)}, f32[36,1]{1,0:T(8,128)S(1)}, u32[]{:S(2)}, u32[]{:S(2)}) collective-permute-start(f32[36,1]{1,0:T(8,128)S(1)} %get-tuple-element.17), channel_id=1, source_target_pairs={{0,1},{1,2},{2,3},{3,4},{4,5},{5,6},{6,7},{7,8},{8,9},{9,10},{10,1... | collective-permute-start | bytes 440 | tf_op jit(solution)/shard_map/ppermute | solution.py:21
  220.0 0.0 collective-permute-done.7
  220.0 4.8 %collective-permute-done.6 = f32[36,1]{1,0:T(8,128)S(1)} collective-permute-done((f32[36,1]{1,0:T(8,128)S(1)}, f32[36,1]{1,0:T(8,128)S(1)}, u32[]{:S(2)}, u32[]{:S(2)}) %collective-permute-start.6) | collective-permute-done | bytes 176 | tf_op jit(solution)/shard_map/ppermute | solution.py:21
  224.8 0.1 select_maximum_fusion
  224.9 0.7 exponential_multiply_fusion
  225.6 0.6 multiply_convert_fusion
  226.2 1.3 copy.15
  227.5 0.0 copy-done.4
  (3 shorter events, 0.0 us)
Async XLA Ops:
  7.2 189.2 %copy-start = (f32[8,8]{1,0:T(8,128)S(1)}, f32[8,8]{1,0:T(8,128)}, u32[]{:S(2)}) copy-start(f32[8,8]{1,0:T(8,128)} %param.13) | copy-start | bytes 772
  7.2 188.0 %all-reduce.6.cloned.1.call-start = ((), (), s32[]{:S(2)}) async-start(), calls=%async_computation | async-start | bytes 1179648 | tf_op jit(solution)/shard_map/psum | solution.py:74
  8.1 103.6 %collective-permute-start.1 = (f32[36,1]{1,0:T(8,128)S(1)}, f32[36,1]{1,0:T(8,128)S(1)}, u32[]{:S(2)}, u32[]{:S(2)}) collective-permute-start(f32[36,1]{1,0:T(8,128)S(1)} %get-tuple-element.22), channel_id=1, source_target_pairs={{1,0},{2,1},{3,2},{4,3},{5,4},{6,5},{7,6},{8,7},{9,8},{10,9},{11,1... | collective-permute-start | bytes 440 | tf_op jit(solution)/shard_map/ppermute | solution.py:24
  10.1 101.6 %collective-permute-start = (f32[36,1]{1,0:T(8,128)S(1)}, f32[36,1]{1,0:T(8,128)S(1)}, u32[]{:S(2)}, u32[]{:S(2)}) collective-permute-start(f32[36,1]{1,0:T(8,128)S(1)} %get-tuple-element.23), channel_id=1, source_target_pairs={{0,1},{1,2},{2,3},{3,4},{4,5},{5,6},{6,7},{7,8},{8,9},{9,10},{10,1... | collective-permute-start | bytes 440 | tf_op jit(solution)/shard_map/ppermute | solution.py:21
  20.1 8.2 %copy-start.3 = (s32[36,128]{1,0:T(8,128)S(1)}, s32[36,128]{1,0:T(8,128)}, u32[]{:S(2)}) copy-start(s32[36,128]{1,0:T(8,128)} %param.9) | copy-start | bytes 55300
  20.1 8.2 %copy-start.6 = (f32[8]{0:T(128)S(1)}, f32[8]{0:T(128)}, u32[]{:S(2)}) copy-start(f32[8]{0:T(128)} %param.15) | copy-start | bytes 100
  20.1 8.2 %copy-start.7 = (f32[8]{0:T(128)S(1)}, f32[8]{0:T(128)}, u32[]{:S(2)}) copy-start(f32[8]{0:T(128)} %param.14) | copy-start | bytes 100
  20.1 91.6 %copy-start.2 = (f32[36,128]{1,0:T(8,128)S(1)}, f32[36,128]{1,0:T(8,128)}, u32[]{:S(2)}) copy-start(f32[36,128]{1,0:T(8,128)} %param.11) | copy-start | bytes 55300
  28.0 168.6 %copy-start.1 = (f32[36,128]{1,0:T(8,128)S(1)}, f32[36,128]{1,0:T(8,128)}, u32[]{:S(2)}) copy-start(f32[36,128]{1,0:T(8,128)} %param.12) | copy-start | bytes 55300
  28.1 168.6 %copy-start.5 = (f32[36,128]{1,0:T(8,128)S(1)}, f32[36,128]{1,0:T(8,128)}, u32[]{:S(2)}) copy-start(f32[36,128]{1,0:T(8,128)} %param.10) | copy-start | bytes 55300
  196.8 30.7 %copy-start.4 = (f32[36,128]{1,0:T(8,128)}, f32[36,128]{1,0:T(8,128)S(1)}, u32[]{:S(2)}) copy-start(f32[36,128]{1,0:T(8,128)S(1)} %get-tuple-element.15) | copy-start | bytes 55300
  196.9 4.3 %collective-permute-start.3 = (f32[36,1]{1,0:T(8,128)S(1)}, f32[36,1]{1,0:T(8,128)S(1)}, u32[]{:S(2)}, u32[]{:S(2)}) collective-permute-start(f32[36,1]{1,0:T(8,128)S(1)} %get-tuple-element.20), channel_id=1, source_target_pairs={{1,0},{2,1},{3,2},{4,3},{5,4},{6,5},{7,6},{8,7},{9,8},{10,9},{11,1... | collective-permute-start | bytes 440 | tf_op jit(solution)/shard_map/ppermute | solution.py:24
  198.8 7.2 %collective-permute-start.2 = (f32[36,1]{1,0:T(8,128)S(1)}, f32[36,1]{1,0:T(8,128)S(1)}, u32[]{:S(2)}, u32[]{:S(2)}) collective-permute-start(f32[36,1]{1,0:T(8,128)S(1)} %get-tuple-element.21), channel_id=1, source_target_pairs={{0,1},{1,2},{2,3},{3,4},{4,5},{5,6},{6,7},{7,8},{8,9},{9,10},{10,1... | collective-permute-start | bytes 440 | tf_op jit(solution)/shard_map/ppermute | solution.py:21
  206.3 4.3 %collective-permute-start.5 = (f32[36,1]{1,0:T(8,128)S(1)}, f32[36,1]{1,0:T(8,128)S(1)}, u32[]{:S(2)}, u32[]{:S(2)}) collective-permute-start(f32[36,1]{1,0:T(8,128)S(1)} %get-tuple-element.18), channel_id=1, source_target_pairs={{1,0},{2,1},{3,2},{4,3},{5,4},{6,5},{7,6},{8,7},{9,8},{10,9},{11,1... | collective-permute-start | bytes 440 | tf_op jit(solution)/shard_map/ppermute | solution.py:24
  208.2 7.2 %collective-permute-start.4 = (f32[36,1]{1,0:T(8,128)S(1)}, f32[36,1]{1,0:T(8,128)S(1)}, u32[]{:S(2)}, u32[]{:S(2)}) collective-permute-start(f32[36,1]{1,0:T(8,128)S(1)} %get-tuple-element.19), channel_id=1, source_target_pairs={{0,1},{1,2},{2,3},{3,4},{4,5},{5,6},{6,7},{7,8},{8,9},{9,10},{10,1... | collective-permute-start | bytes 440 | tf_op jit(solution)/shard_map/ppermute | solution.py:21
  215.7 4.3 %collective-permute-start.7 = (f32[36,1]{1,0:T(8,128)S(1)}, f32[36,1]{1,0:T(8,128)S(1)}, u32[]{:S(2)}, u32[]{:S(2)}) collective-permute-start(f32[36,1]{1,0:T(8,128)S(1)} %get-tuple-element.16), channel_id=1, source_target_pairs={{1,0},{2,1},{3,2},{4,3},{5,4},{6,5},{7,6},{8,7},{9,8},{10,9},{11,1... | collective-permute-start | bytes 440 | tf_op jit(solution)/shard_map/ppermute | solution.py:24
  217.6 7.2 %collective-permute-start.6 = (f32[36,1]{1,0:T(8,128)S(1)}, f32[36,1]{1,0:T(8,128)S(1)}, u32[]{:S(2)}, u32[]{:S(2)}) collective-permute-start(f32[36,1]{1,0:T(8,128)S(1)} %get-tuple-element.17), channel_id=1, source_target_pairs={{0,1},{1,2},{2,3},{3,4},{4,5},{5,6},{6,7},{7,8},{8,9},{9,10},{10,1... | collective-permute-start | bytes 440 | tf_op jit(solution)/shard_map/ppermute | solution.py:21
Sparse Core Ops, SparseCore 0:
  20.2 174.9 all-reduce.5
where the time goes:
time: 235 us; the launch traced here: 234 us
  waiting for transfers between devices  97.7 us (42%)
  blocking collectives  83.3 us (35%)
  starting transfers between devices  17.3 us (7%)
  between operations  14.3 us (6%)
  other arithmetic  11.5 us (5%)
  local copies, waits for them, and re-layouts  8.36 us (4%)
    psum x1, waiting for transfers between devices, per_device(): coeffs = lax.psum(partial_sums, 'circ') * scale  83.3 us
    pmax x1, blocking collectives, per_device(): top = lax.pmax(jnp.max(energy, axis=0), 'circ')  83.3 us
    ppermute x4, waiting for transfers between devices, extended_2(): lax.ppermute(lax.slice_in_dim(block, block.shape[dim] - width, None, axis...  14.4 us
    ppermute x4, starting transfers between devices, extended_2(): lax.ppermute(lax.slice_in_dim(block, block.shape[dim] - width, None, axis...  9.53 us
    reduce_sum x1, other arithmetic, per_device(): energy = jnp.sum(jnp.square(strain.astype(jnp.float32)), axis=1)  7.91 us
    ppermute x4, starting transfers between devices, extended_2(): lax.ppermute(lax.slice_in_dim(block, 0, width, axis=dim), axis, backward)  7.74 us
    unnamed x18, local copies, waits for them, and re-layouts  7.26 us
  transfers between devices with their start and end apart: 9, of which 4 were waited for; matrix products, arithmetic and copies ran while one was open for 7% of the time, Pallas kernels for 0%

commit v1 on v0

v1 whole, which is shorter than its diff:
```python
import functools
import math

import jax
import jax.numpy as jnp
import ml_dtypes
import numpy as np
from jax import lax
from jax.experimental import pallas as pl
from jax.experimental.pallas import tpu as pltpu
from jax.sharding import PartitionSpec as P

COMP = 2
HARM = 8
SWEEPS = 4
SINK = 0.1
SEC = 128
LAY = 36
LANES = 128
NREG = 8
CIRC = 16
NSEC = SEC * CIRC
RANK = 10
ROWS = 48
EDGE = 4
FIELD_ROWS = 40


def split3(values):
    parts = []
    rest = values.astype(np.float64)
    for _ in range(3):
        part = rest.astype(ml_dtypes.bfloat16)
        parts.append(part)
        rest = rest - part.astype(np.float64)
    return parts


def window_basis():
    t = (np.arange(SEC) - 0.5 * (SEC - 1)) / (0.5 * (SEC - 1))
    rows = [np.ones_like(t), t]
    for _ in range(RANK - 2):
        rows.append(2.0 * t * rows[-1] - rows[-2])
    return np.stack(rows)


def project_matrix():
    basis = window_basis()
    full = np.zeros((COMP * RANK, SEC, COMP))
    for comp in range(COMP):
        full[comp * RANK : (comp + 1) * RANK, :, comp] = basis
    full = full.reshape(COMP * RANK, SEC * COMP)
    out = []
    for kind in range(3):
        rows = np.zeros((32 if kind == 2 else 24, SEC * COMP))
        if kind == 0:
            rows[:20] = full
        elif kind == 1:
            rows[4:] = full
        else:
            for b in range(4):
                rows[8 * b : 8 * b + 5] = full[5 * b : 5 * b + 5]
        out.append(np.concatenate(split3(rows)))
    return np.concatenate(out)


def combine_matrix():
    half = 0.5 * (SEC - 1) * 2.0 * math.pi / NSEC
    nodes = 64
    n = (np.arange(nodes) + 0.5) * math.pi / nodes
    even = np.zeros((HARM, RANK))
    odd = np.zeros((HARM, RANK))
    for k in range(1, HARM + 1):
        for m in range(RANK):
            weight = (1.0 if m == 0 else 2.0) / nodes
            f = np.cos(k * half * np.cos(n)) if m % 2 == 0 else np.sin(k * half * np.cos(n))
            (even if m % 2 == 0 else odd)[k - 1, m] = weight * np.sum(f * np.cos(m * n))
    u = np.zeros((2 * HARM, CIRC, RANK))
    for d in range(CIRC):
        centre = 2.0 * math.pi * (SEC * d + 0.5 * (SEC - 1)) / NSEC
        for k in range(1, HARM + 1):
            c, s = math.cos(k * centre), math.sin(k * centre)
            u[k - 1, d] = c * even[k - 1] - s * odd[k - 1]
            u[HARM + k - 1, d] = s * even[k - 1] + c * odd[k - 1]
    u = u / math.sqrt(NSEC)
    w = np.zeros((128, CIRC, ROWS))
    for a in range(2):
        for comp in range(COMP):
            at = 20 * a + RANK * comp
            w[32 * a + 16 * comp : 32 * a + 16 * comp + 16, :, at : at + RANK] = u
    for b in range(4):
        first = 5 * (b % 2)
        w[64 + 16 * b : 64 + 16 * b + 16, :, 40:45] = u[:, :, first : first + 5]
    w = w.reshape(128, CIRC * ROWS)
    hi = w.astype(ml_dtypes.bfloat16)
    lo = (w - hi.astype(np.float64)).astype(ml_dtypes.bfloat16)
    return np.concatenate([hi, lo])


def lane_of(shape):
    return lax.broadcasted_iota(jnp.int32, shape, len(shape) - 1)


def row_of(shape):
    return lax.broadcasted_iota(jnp.int32, shape, 0)


def halves(first, second):
    low = lane_of(first.shape) < 64
    return (
        jnp.where(low, first, pltpu.roll(second, 64, 1)),
        jnp.where(low, pltpu.roll(first, 64, 1), second),
    )


def quarter_of(u, h):
    return 3 * h if u % 2 == 0 else 1 + h


CHUNK = 12


def project_kernel(strain_hbm, a_ref, send_ref, energy_ref, buf, squares, sem):
    copies = [
        pltpu.make_async_copy(strain_hbm.at[:, l], buf.at[l], sem.at[l]) for l in range(LAY)
    ]
    for copy in copies:
        copy.start()
    rows = buf.reshape(LAY, SEC * COMP, LANES)
    tops = {}
    sums = {}
    sub = row_of((8, LANES))
    block = lane_of((8, LANES)) // 32

    def pair(t):
        kind = 2 if t >= 16 else t % 2
        size = 32 if kind == 2 else 24
        base = 72 * kind
        x = jnp.concatenate([rows[2 * t], rows[2 * t + 1]], axis=1)
        d = jnp.dot(a_ref[base : base + 3 * size], x, preferred_element_type=jnp.float32)
        d = d[:size] + d[size : 2 * size] + d[2 * size :]
        for i in range(2):
            l = 2 * t + i
            slot = l % CHUNK
            wide = rows[l].astype(jnp.float32)
            squares[slot] = wide * wide
            e = squares[slot, pl.ds(0, SEC, stride=2), :] + squares[slot, pl.ds(1, SEC, stride=2), :]
            energy_ref[l] = e
            tops[l] = jnp.max(e, axis=0, keepdims=True)
            sums[l] = d[:, LANES * i : LANES * (i + 1)]

    for l in range(LAY):
        if l % CHUNK == 0:
            for other in range(l, min(l + CHUNK, LAY)):
                copies[other].wait()
        if l % 2 == 0:
            pair(l // 2)

    tails = {}
    for v in range(4):
        x = sums[32 + v]
        shifted = []
        for delta in range(4):
            w = jnp.zeros((8, LANES), jnp.float32)
            for b in range(4):
                w = jnp.where(block == (b - delta) % 4, x[8 * b : 8 * b + 8], w)
            shifted.append(pltpu.roll(w, 32 * delta, 1) if delta else w)
        for g in range(4):
            y = shifted[0]
            for b in range(4):
                y = jnp.where(block == b, shifted[(b - g) % 4], y)
            tails[v, g] = y

    for u in range(8):
        first = halves(sums[4 * u], sums[4 * u + 1])
        second = halves(sums[4 * u + 2], sums[4 * u + 3])
        top0 = halves(tops[4 * u], tops[4 * u + 1])
        top1 = halves(tops[4 * u + 2], tops[4 * u + 3])
        for h in range(2):
            c = 2 * u + h
            v, g = u // 2, quarter_of(u, h)
            send_ref[c, 0:16] = first[h][0:16]
            send_ref[c, 16:24] = first[h][16:24] + second[h][0:8]
            send_ref[c, 24:40] = second[h][8:24]
            top2 = tops[32 + v]
            if g:
                top2 = pltpu.roll(top2, LANES - 32 * g, 1)
            tile = jnp.where(sub == 5, top0[h], tails[v, g])
            tile = jnp.where(sub == 6, top1[h], tile)
            send_ref[c, 40:48] = jnp.where(sub == 7, top2, tile)


def project(strain, a):
    return pl.pallas_call(
        project_kernel,
        name="project",
        out_shape=[
            jax.ShapeDtypeStruct((CIRC, ROWS, LANES), jnp.float32),
            jax.ShapeDtypeStruct((LAY, SEC, LANES), jnp.float32),
        ],
        in_specs=[pl.BlockSpec(memory_space=pl.ANY), pl.BlockSpec(memory_space=pltpu.VMEM)],
        out_specs=[pl.BlockSpec(memory_space=pltpu.VMEM)] * 2,
        scratch_shapes=[
            pltpu.VMEM((LAY, SEC, COMP, LANES), jnp.bfloat16),
            pltpu.VMEM((CHUNK, SEC * COMP, LANES), jnp.float32),
            pltpu.SemaphoreType.DMA((LAY,)),
        ],
        compiler_params=pltpu.CompilerParams(vmem_limit_bytes=32 * 2**20),
    )(strain, a)


def owner_kernel(
    recv_ref, w_ref, region_ref, prior_ref, temp_ref, cond_ref, loss_ref, mullins_ref, own_ref, msg_ref
):
    c = lax.axis_index("circ")
    u = c // 2
    h = c % 2
    is_left = h == 0
    lane = lane_of((1, LANES))
    sub = row_of((8, LANES))
    p = recv_ref[...]
    hi = p.astype(jnp.bfloat16)
    lo = (p - hi.astype(jnp.float32)).astype(jnp.bfloat16)
    o = jnp.dot(
        w_ref[...], jnp.concatenate([hi, lo], axis=1), preferred_element_type=jnp.float32
    )
    coeffs = o[:128, :LANES] + o[128:, :LANES] + o[:128, LANES:]
    squared = coeffs[:64] * coeffs[:64]
    powers = [
        squared[32 * a : 32 * a + 8]
        + squared[32 * a + 8 : 32 * a + 16]
        + squared[32 * a + 16 : 32 * a + 24]
        + squared[32 * a + 24 : 32 * a + 32]
        for a in range(2)
    ]
    last = [coeffs[64 + 16 * b : 80 + 16 * b] for b in range(4)]
    comp0 = last[0] + pltpu.roll(last[1], 96, 1)
    comp1 = pltpu.roll(last[2], 64, 1) + pltpu.roll(last[3], 32, 1)
    comp0, comp1 = comp0 * comp0, comp1 * comp1
    powers.append(comp0[:8] + comp0[8:] + comp1[:8] + comp1[8:])

    quarter = jnp.where(u % 2 == 0, 3 * h, 1 + h)
    back = (LANES - 32 * quarter) % LANES

    def natural(ref):
        rows = [ref[pl.ds(4 * u + j, 1), :] for j in range(4)]
        rows.append(ref[pl.ds(32 + u // 2, 1), :])
        return rows

    def packed(rows):
        out = []
        for a in range(2):
            left, right = halves(rows[2 * a], rows[2 * a + 1])
            out.append(jnp.where(is_left, left, right))
        out.append(pltpu.roll(rows[4], back, 1))
        return out

    region = packed(natural(region_ref))
    prior = packed(natural(prior_ref))
    temp_rows = natural(temp_ref)
    temp = packed(temp_rows)
    cond_rows = natural(cond_ref)
    heats, peaks = [], []
    for i in range(3):
        q = loss_ref[:, 0:1] * powers[i][0:1]
        for k in range(1, HARM):
            q = q + loss_ref[:, k : k + 1] * powers[i][k : k + 1]
        picked = jnp.sum(jnp.where(region[i] == sub, q, 0.0), axis=0, keepdims=True)
        share = jnp.zeros((1, LANES), jnp.float32)
        for r in range(NREG):
            share = jnp.where(region[i] == r, mullins_ref[0:1, r : r + 1], share)
        top = jnp.max(recv_ref[pl.ds(45 + i, CIRC, stride=ROWS), :], axis=0, keepdims=True)
        peak = jnp.maximum(prior[i], top)
        heats.append(jnp.exp(-0.5 * temp[i]) * picked + share * (peak - prior[i]))
        peaks.append(peak)

    third = (lane >= 32) & (lane < 64)
    own = jnp.where(sub == 0, heats[0], 0.0)
    own = jnp.where(sub == 1, heats[1], own)
    own = jnp.where(sub == 2, peaks[0], own)
    own = jnp.where(sub == 3, peaks[1], own)
    own = jnp.where((sub == 4) & third, pltpu.roll(heats[2], 32, 1), own)
    own_ref[...] = jnp.where((sub == 5) & third, pltpu.roll(peaks[2], 32, 1), own)

    edge_heat = []
    for a in range(2):
        turned = pltpu.roll(heats[a], 64, 1)
        edge_heat.append(jnp.where(is_left, heats[a], turned))
        edge_heat.append(jnp.where(is_left, turned, heats[a]))
    edge_heat.append(jnp.where(is_left, heats[2], pltpu.roll(heats[2], 96, 1)))
    edge = jnp.where(is_left, lane, LANES - 1 - lane) < EDGE
    step = jnp.where(is_left, EDGE, LANES - EDGE)
    msg = jnp.zeros((8, LANES), jnp.float32)
    for j in range(5):
        row = jnp.where(edge, edge_heat[j], 0.0)
        row = row + pltpu.roll(jnp.where(edge, cond_rows[j], 0.0), step, 1)
        row = row + pltpu.roll(jnp.where(edge, temp_rows[j], 0.0), (2 * step) % LANES, 1)
        if j < 4:
            msg = msg + jnp.where(sub == 4 + j, row, 0.0)
        else:
            row = pltpu.roll(row, jnp.where(is_left, 32, 96), 1)
            msg = msg + jnp.where(sub == 6, row, 0.0)
    msg_ref[...] = msg


def owner(recv, w, region, prior, temp, cond, loss, mullins):
    vmem = pl.BlockSpec(memory_space=pltpu.VMEM)
    return pl.pallas_call(
        owner_kernel,
        name="owner",
        out_shape=[jax.ShapeDtypeStruct((8, LANES), jnp.float32)] * 2,
        in_specs=[vmem] * 8,
        out_specs=[vmem] * 2,
        compiler_params=pltpu.CompilerParams(vmem_limit_bytes=32 * 2**20),
    )(recv, w, region, prior, temp, cond, loss, mullins)


GROUPS = 6


def modulus_kernel(
    all_ref, energy_ref, region_ref, temp_ref, cond_ref, stiff_ref,
    field_hbm, peak_hbm, out_hbm,
    heat_s, peak_s, halo_s, cond_s, temp_s, region_s, field_s, out_s, sem,
):
    low = lane_of((8, LANES)) < 64
    lane = lane_of((FIELD_ROWS, LANES))
    for scratch in (heat_s, peak_s, halo_s, cond_s, temp_s):
        scratch[32:FIELD_ROWS] = jnp.zeros((8, LANES), jnp.float32)
    region_s[32:FIELD_ROWS] = jnp.zeros((8, LANES), jnp.int32)
    cond_s[0:LAY] = cond_ref[...]
    temp_s[0:LAY] = temp_ref[...]
    region_s[0:LAY] = region_ref[...]
    for a in range(2):
        for base, target in ((0, heat_s), (2, peak_s)):
            left = all_ref[pl.ds(base + a, 8, stride=16), :]
            right = all_ref[pl.ds(8 + base + a, 8, stride=16), :]
            target[pl.ds(2 * a, 8, stride=4), :] = jnp.where(low, left, pltpu.roll(right, 64, 1))
            target[pl.ds(2 * a + 1, 8, stride=4), :] = jnp.where(low, pltpu.roll(left, 64, 1), right)
    small = lane_of((4, LANES))
    for base, target in ((4, heat_s), (5, peak_s)):
        row = jnp.zeros((4, LANES), jnp.float32)
        for odd, h, g in ((0, 0, 0), (1, 0, 1), (1, 1, 2), (0, 1, 3)):
            part = all_ref[pl.ds(16 * odd + 8 * h + base, 4, stride=32), :]
            if g != 1:
                part = pltpu.roll(part, (32 * g - 32) % LANES, 1)
            row = jnp.where(small // 32 == g, part, row)
        target[32:LAY] = row
    wide = lane_of((8, LANES))
    outer = (wide < 3 * EDGE) | (wide >= LANES - 3 * EDGE)
    for j in range(4):
        both = all_ref[pl.ds(4 + j, 8, stride=16), :] + all_ref[pl.ds(12 + j, 8, stride=16), :]
        halo_s[pl.ds(j, 8, stride=4), :] = jnp.where(outer, both, 0.0)
    from_left = pltpu.roll(all_ref[pl.ds(6, 4, stride=32), :], 32, 1)
    from_right = pltpu.roll(all_ref[pl.ds(14, 4, stride=32), :], 96, 1)
    halo_s[32:LAY] = jnp.where(
        small >= LANES - 3 * EDGE, from_left, jnp.where(small < 3 * EDGE, from_right, 0.0)
    )

    halo = halo_s[...]

    def unpack(n):
        low_part = pltpu.roll(halo, (LANES - EDGE * n) % LANES, 1) if n else halo
        high_part = pltpu.roll(halo, EDGE * n, 1) if n else halo
        return jnp.where(
            lane < EDGE, low_part, jnp.where(lane >= LANES - EDGE, high_part, 0.0)
        )

    peak = peak_s[...]
    heat = (heat_s[...], unpack(0))
    cond = (cond_s[...], unpack(1))
    field = (temp_s[...], unpack(2))
    scale = [1.0 / (4.0 * k + SINK) for k in cond]
    heat = [x * y for x, y in zip(heat, scale)]
    cond = [x * y for x, y in zip(cond, scale)]
    rows = row_of((FIELD_ROWS, LANES))
    valid = rows < LAY
    first, final = lane == 0, lane == LANES - 1
    for _ in range(SWEEPS):
        right = [pltpu.roll(x, 1, 1) for x in field]
        left = [pltpu.roll(x, LANES - 1, 1) for x in field]
        new = []
        for i in range(2):
            beside = jnp.where(first, right[1 - i], right[i]) + jnp.where(final, left[1 - i], left[i])
            beside = beside + pltpu.roll(field[i], 1, 0) + pltpu.roll(field[i], FIELD_ROWS - 1, 0)
            new.append(jnp.where(valid, heat[i] + cond[i] * beside, 0.0))
        field = new
    field_s[...] = field[0]
    copies = [
        pltpu.make_async_copy(field_s.at[0:LAY], field_hbm, sem.at[0]),
        pltpu.make_async_copy(peak_s.at[0:LAY], peak_hbm, sem.at[1]),
    ]
    for copy in copies:
        copy.start()
    region = region_s[...]
    stiff = jnp.zeros((FIELD_ROWS, LANES), jnp.float32)
    for r in range(NREG):
        stiff = jnp.where(region == r, stiff_ref[0:1, r : r + 1], stiff)
    factor = stiff * jnp.exp(-0.5 * field[0])
    size = LAY // GROUPS
    for group in range(GROUPS):
        for l in range(group * size, (group + 1) * size):
            soft = jnp.tanh((peak[l : l + 1] - energy_ref[l]) * 0.25)
            out_s[l] = (factor[l : l + 1] * (1.0 - 0.5 * soft)).astype(jnp.bfloat16)
        where = pl.ds(group * size, size)
        copy = pltpu.make_async_copy(out_s.at[where], out_hbm.at[where], sem.at[2 + group])
        copy.start()
        copies.append(copy)
    for copy in copies:
        copy.wait()


def soften(everything, energy, region, temp, cond, stiff):
    vmem = pl.BlockSpec(memory_space=pltpu.VMEM)
    plane = pltpu.VMEM((FIELD_ROWS, LANES), jnp.float32)
    return pl.pallas_call(
        modulus_kernel,
        name="modulus",
        out_shape=[
            jax.ShapeDtypeStruct((LAY, LANES), jnp.float32),
            jax.ShapeDtypeStruct((LAY, LANES), jnp.float32),
            jax.ShapeDtypeStruct((LAY, SEC, LANES), jnp.bfloat16),
        ],
        in_specs=[vmem] * 6,
        out_specs=[pl.BlockSpec(memory_space=pl.ANY)] * 3,
        scratch_shapes=[
            plane, plane, plane, plane, plane,
            pltpu.VMEM((FIELD_ROWS, LANES), jnp.int32),
            plane,
            pltpu.VMEM((LAY, SEC, LANES), jnp.bfloat16),
            pltpu.SemaphoreType.DMA((2 + GROUPS,)),
        ],
        compiler_params=pltpu.CompilerParams(vmem_limit_bytes=32 * 2**20),
    )(everything, energy, region, temp, cond, stiff)


def per_device(sects, a, w, strain, region, prior, temp, cond, loss, mullins, stiff):
    send, energy = project(strain.transpose(0, 2, 1, 3), a)
    recv = lax.all_to_all(send, "circ", 0, 0, tiled=True)
    own, msg = owner(
        recv.reshape(CIRC * ROWS, LANES), w, region, prior, temp, cond, loss, mullins.reshape(1, NREG)
    )
    pairs = []
    for s in range(1, sects):
        for u in range(CIRC // 2):
            left, right = 2 * u * sects + s, (2 * u + 1) * sects + s - 1
            pairs += [(left, right), (right, left)]
    halo = lax.ppermute(msg, ("circ", "sect"), pairs)
    block = jnp.broadcast_to((own + halo)[None], (CIRC, 8, LANES))
    everything = lax.all_to_all(block, "circ", 0, 0, tiled=True)
    field, peak, modulus = soften(
        everything.reshape(CIRC * 8, LANES), energy, region, temp, cond, stiff.reshape(1, NREG)
    )
    return field, peak, modulus.transpose(1, 0, 2)


def solution(mesh):
    a = project_matrix()
    w = combine_matrix()
    maps = P(None, "sect")

    def whole(*args):
        return jax.shard_map(
            functools.partial(per_device, mesh.shape["sect"], jnp.asarray(a), jnp.asarray(w)),
            mesh=mesh,
            in_specs=(P("circ", None, None, "sect"), maps, maps, maps, maps, P(), P(), P()),
            out_specs=(maps, maps, P("circ", None, "sect")),
            check_vma=False,
        )(*args)

    return whole
```

time: 235 us -> 59.4 us (0.25)
  waiting for transfers between devices: 97.7 us -> 6.01 us
  blocking collectives: 83.3 us -> 38.9 us
  starting transfers between devices: 17.3 us -> 1.91 us
  between operations: 14.3 us -> 0.73 us
  other arithmetic: 11.5 us -> 0.01 us
  Pallas kernels: 0 us -> 9.02 us
  local copies, waits for them, and re-layouts: 8.36 us -> 2.61 us
    psum x1 -> x0, waiting for transfers between devices: 83.3 us -> none  [per_device(): coeffs = lax.psum(partial_sums, 'circ') * scale]
    pmax x1 -> x0, blocking collectives: 83.3 us -> none  [per_device(): top = lax.pmax(jnp.max(energy, axis=0), 'circ')]
    all_to_all x0 -> x2, blocking collectives: none -> 38.9 us  [the longest x1 24.4 us: per_device(): recv = lax.all_to_all(send, 'circ', 0, 0, tiled=True)]
    ppermute x8 -> x1, starting transfers between devices: 17.3 us -> 1.91 us  [per_device(): halo = lax.ppermute(msg, ('circ', 'sect'), pairs)]
    pallas_call x0 -> x3, Pallas kernels: none -> 9.02 us  [the longest x1 6.52 us: project(): pl.pallas_call(project_kernel, name='project', out_shape=[jax.ShapeDtypeS...]
    ppermute x8 -> x1, waiting for transfers between devices: 14.4 us -> 6.01 us  [per_device(): halo = lax.ppermute(msg, ('circ', 'sect'), pairs)]
    reduce_sum x3 -> x0, other arithmetic: 8.11 us -> none  [the longest x1 7.91 us: per_device(): energy = jnp.sum(jnp.square(strain.astype(jnp.float32)), axis=1)]
    unnamed x18 -> x20, local copies, waits for them, and re-layouts: 7.26 us -> 2.6 us
  transfers between devices with their start and end apart: 9 -> 1, of which waited for: 4 -> 1; matrix products, arithmetic and copies ran while one was open for 7% -> 0% of each run, Pallas kernels for 0% -> 0%
where the time goes in v1:
time: 59.4 us; the launch traced here: 59.2 us
  blocking collectives  38.9 us (65%)
  Pallas kernels  9.02 us (15%)
  waiting for transfers between devices  6.01 us (10%)
  local copies, waits for them, and re-layouts  2.61 us (4%)
  starting transfers between devices  1.91 us (3%)
  between operations  0.73 us (1%)
    all_to_all x1, blocking collectives, per_device(): recv = lax.all_to_all(send, 'circ', 0, 0, tiled=True)  24.4 us
    all_to_all x1, blocking collectives, per_device(): everything = lax.all_to_all(block, 'circ', 0, 0, tiled=True)  14.5 us
    pallas_call x1, Pallas kernels, project(): pl.pallas_call(project_kernel, name='project', out_shape=[jax.ShapeDtypeS...  6.52 us
    ppermute x1, waiting for transfers between devices, per_device(): halo = lax.ppermute(msg, ('circ', 'sect'), pairs)  6.01 us
    unnamed x20, local copies, waits for them, and re-layouts  2.6 us
    pallas_call x1, Pallas kernels, soften(): pl.pallas_call(modulus_kernel, name='modulus', out_shape=[jax.ShapeDtypeS...  1.98 us
    ppermute x1, starting transfers between devices, per_device(): halo = lax.ppermute(msg, ('circ', 'sect'), pairs)  1.91 us
  transfers between devices with their start and end apart: 1, of which 1 were waited for; matrix products, arithmetic and copies ran while one was open for 0% of the time, Pallas kernels for 0%

profile of v1, /device:TPU:256, one launch (start us, length us, event | category | flops | bytes accessed | tf_op | source)
XLA Modules:
  0.0 59.2 jit_solution(4772042870909277742)
XLA Ops:
  0.6 0.0 copy-start.8
  0.6 0.0 copy-start.9
  0.7 0.0 copy-start
  0.7 1.7 %copy-done = bf16[128,2,36,128]{3,1,2,0:T(2,128)(2,1)S(1)} copy-done((bf16[128,2,36,128]{3,1,2,0:T(2,128)(2,1)S(1)}, bf16[128,2,36,128]{3,1,2,0:T(2,128)(2,1)}, u32[]{:S(2)}) %copy-start) | copy-done | bytes 2359320
  2.3 0.0 copy-start.2
  2.3 0.9 %copy-done.2 = bf16[240,256]{1,0:T(8,128)(2,1)S(1)} copy-done((bf16[240,256]{1,0:T(8,128)(2,1)S(1)}, bf16[240,256]{1,0:T(8,128)(2,1)}, u32[]{:S(2)}) %copy-start.2) | copy-done | bytes 122904
  3.2 0.0 copy-start.1
  3.2 0.0 copy-start.3
  3.2 0.0 copy-start.4
  3.2 0.0 copy-start.5
  3.2 0.0 copy-start.6
  3.3 0.0 copy-start.7
  3.3 6.5 %project.1 = (f32[16,48,128]{2,1,0:T(8,128)S(1)}, f32[36,128,128]{2,1,0:T(8,128)S(1)}) custom-call(bf16[128,36,2,128]{3,2,1,0:T(2,128)(2,1)S(1)} %bitcast.6, bf16[240,256]{1,0:T(8,128)(2,1)S(1)} %copy-done.2), custom_call_target="tpu_custom_call" | custom-call | tf_op jit(solution)/shard_map/project/pallas_call | solution.py:194
  9.8 24.4 %all_to_all.10 = f32[16,48,128]{2,1,0:T(8,128)S(1)} all-to-all(f32[16,48,128]{2,1,0:T(8,128)S(1)} %get-tuple-element.10), channel_id=1, replica_groups=mesh['circ'=16,'sect'=32] {'circ'}, dimensions={0} | all-to-all | bytes 786432 | tf_op jit(solution)/shard_map/all_to_all | solution.py:439
  34.2 0.0 copy-done.8
  34.2 0.0 copy-done.1
  34.2 0.0 copy-done.3
  34.2 0.0 copy-done.4
  34.2 0.0 copy-done.5
  34.2 0.0 copy-done.6
  34.2 0.0 copy-done.7
  34.2 0.5 owner.1
  34.8 1.9 %collective-permute-start = (f32[8,128]{1,0:T(8,128)S(1)}, f32[8,128]{1,0:T(8,128)S(1)}, u32[]{:S(2)}, u32[]{:S(2)}) collective-permute-start(f32[8,128]{1,0:T(8,128)S(1)} %get-tuple-element.12), channel_id=1, source_target_pairs={{1,32},{32,1},{65,96},{96,65},{129,160},{160,129},{193,224},{224,1... | collective-permute-start | bytes 12296 | tf_op jit(solution)/shard_map/ppermute | solution.py:448
  36.7 6.0 %collective-permute-done = f32[8,128]{1,0:T(8,128)S(1)} collective-permute-done((f32[8,128]{1,0:T(8,128)S(1)}, f32[8,128]{1,0:T(8,128)S(1)}, u32[]{:S(2)}, u32[]{:S(2)}) %collective-permute-start) | collective-permute-done | bytes 4128 | tf_op jit(solution)/shard_map/ppermute | solution.py:448
  42.7 14.5 %all_to_all.11 = f32[16,8,128]{2,1,0:T(8,128)S(1)} all-to-all(f32[16,8,128]{2,1,0:T(8,128)S(1)} %broadcast_in_dim.2), channel_id=1, replica_groups=mesh['circ'=16,'sect'=32] {'circ'}, dimensions={0} | all-to-all | bytes 131072 | tf_op jit(solution)/shard_map/all_to_all | solution.py:450
  57.2 0.0 copy-done.9
  57.2 2.0 %modulus.1 = (f32[36,128]{1,0:T(8,128)}, f32[36,128]{1,0:T(8,128)}, bf16[36,128,128]{2,1,0:T(8,128)(2,1)}) custom-call(f32[128,128]{1,0:T(8,128)S(1)} %bitcast.8, f32[36,128,128]{2,1,0:T(8,128)S(1)} %get-tuple-element.13.energy_ref, s32[36,128]{1,0:T(8,128)S(1)} %copy-done.3, f32[36,128]{1,0:T(8,128)S(1)} %copy-done.4, f32[36,128]{1,0:T(8,128)S(1)} %copy-done.5, ...), custom_call_target="tpu_custom_call" | custom-call | tf_op jit(solution)/shard_map/modulus/pallas_call | solution.py:416
  (2 shorter events, 0.0 us)
Async XLA Ops:
  0.6 33.6 %copy-start.8 = (f32[8]{0:T(128)S(1)}, f32[8]{0:T(128)}, u32[]{:S(2)}) copy-start(f32[8]{0:T(128)} %param.16) | copy-start | bytes 100
  0.6 56.6 %copy-start.9 = (f32[8]{0:T(128)S(1)}, f32[8]{0:T(128)}, u32[]{:S(2)}) copy-start(f32[8]{0:T(128)} %param.17) | copy-start | bytes 100
  0.7 1.7 %copy-start = (bf16[128,2,36,128]{3,1,2,0:T(2,128)(2,1)S(1)}, bf16[128,2,36,128]{3,1,2,0:T(2,128)(2,1)}, u32[]{:S(2)}) copy-start(bf16[128,2,36,128]{3,1,2,0:T(2,128)(2,1)} %param.10) | copy-start | bytes 7077892
  2.3 0.9 %copy-start.2 = (bf16[240,256]{1,0:T(8,128)(2,1)S(1)}, bf16[240,256]{1,0:T(8,128)(2,1)}, u32[]{:S(2)}) copy-start(bf16[240,256]{1,0:T(8,128)(2,1)} %constant.4.clone.a_ref) | copy-start | bytes 368644
  3.2 31.0 %copy-start.1 = (bf16[256,768]{1,0:T(8,128)(2,1)S(1)}, bf16[256,768]{1,0:T(8,128)(2,1)}, u32[]{:S(2)}) copy-start(bf16[256,768]{1,0:T(8,128)(2,1)} %constant.5.clone.w_ref) | copy-start | bytes 1179652
  3.2 31.0 %copy-start.3 = (s32[36,128]{1,0:T(8,128)S(1)}, s32[36,128]{1,0:T(8,128)}, u32[]{:S(2)}) copy-start(s32[36,128]{1,0:T(8,128)} %region_ref.3) | copy-start | bytes 55300
  3.2 31.0 %copy-start.4 = (f32[36,128]{1,0:T(8,128)S(1)}, f32[36,128]{1,0:T(8,128)}, u32[]{:S(2)}) copy-start(f32[36,128]{1,0:T(8,128)} %temp_ref.3) | copy-start | bytes 55300
  3.2 31.0 %copy-start.5 = (f32[36,128]{1,0:T(8,128)S(1)}, f32[36,128]{1,0:T(8,128)}, u32[]{:S(2)}) copy-start(f32[36,128]{1,0:T(8,128)} %cond_ref.3) | copy-start | bytes 55300
  3.2 31.0 %copy-start.6 = (f32[36,128]{1,0:T(8,128)S(1)}, f32[36,128]{1,0:T(8,128)}, u32[]{:S(2)}) copy-start(f32[36,128]{1,0:T(8,128)} %prior_ref.1) | copy-start | bytes 55300
  3.3 31.0 %copy-start.7 = (f32[8,8]{1,0:T(8,128)S(1)}, f32[8,8]{1,0:T(8,128)}, u32[]{:S(2)}) copy-start(f32[8,8]{1,0:T(8,128)} %loss_ref.1) | copy-start | bytes 772
  34.8 7.9 %collective-permute-start = (f32[8,128]{1,0:T(8,128)S(1)}, f32[8,128]{1,0:T(8,128)S(1)}, u32[]{:S(2)}, u32[]{:S(2)}) collective-permute-start(f32[8,128]{1,0:T(8,128)S(1)} %get-tuple-element.12), channel_id=1, source_target_pairs={{1,32},{32,1},{65,96},{96,65},{129,160},{160,129},{193,224},{224,1... | collective-permute-start | bytes 12296 | tf_op jit(solution)/shard_map/ppermute | solution.py:448

commit v2 on v1

--- a/solution.py
+++ b/solution.py
@@ -24,44 +24,6 @@
 ROWS = 48
 EDGE = 4
 FIELD_ROWS = 40
-
-
-def split3(values):
-    parts = []
-    rest = values.astype(np.float64)
-    for _ in range(3):
-        part = rest.astype(ml_dtypes.bfloat16)
-        parts.append(part)
-        rest = rest - part.astype(np.float64)
-    return parts
-
-
-def window_basis():
-    t = (np.arange(SEC) - 0.5 * (SEC - 1)) / (0.5 * (SEC - 1))
-    rows = [np.ones_like(t), t]
-    for _ in range(RANK - 2):
-        rows.append(2.0 * t * rows[-1] - rows[-2])
-    return np.stack(rows)
-
-
-def project_matrix():
-    basis = window_basis()
-    full = np.zeros((COMP * RANK, SEC, COMP))
-    for comp in range(COMP):
-        full[comp * RANK : (comp + 1) * RANK, :, comp] = basis
-    full = full.reshape(COMP * RANK, SEC * COMP)
-    out = []
-    for kind in range(3):
-        rows = np.zeros((32 if kind == 2 else 24, SEC * COMP))
-        if kind == 0:
-            rows[:20] = full
-        elif kind == 1:
-            rows[4:] = full
-        else:
-            for b in range(4):
-                rows[8 * b : 8 * b + 5] = full[5 * b : 5 * b + 5]
-        out.append(np.concatenate(split3(rows)))
-    return np.concatenate(out)
 
 
 def combine_matrix():
@@ -117,18 +79,50 @@
     return 3 * h if u % 2 == 0 else 1 + h
 
 
-CHUNK = 12
-
-
-def project_kernel(strain_hbm, a_ref, send_ref, energy_ref, buf, squares, sem):
-    copies = [
-        pltpu.make_async_copy(strain_hbm.at[:, l], buf.at[l], sem.at[l]) for l in range(LAY)
+def window_matrix():
+    wide = (1, SEC * COMP)
+    lane = lane_of(wide)
+    t = ((lane // 2).astype(jnp.float32) - 0.5 * (SEC - 1)) * (2.0 / (SEC - 1))
+    basis = [jnp.ones(wide, jnp.float32), t]
+    for _ in range(RANK - 2):
+        basis.append(2.0 * t * basis[-1] - basis[-2])
+    rows = [
+        jnp.where(lane % 2 == comp, values, 0.0) for comp in range(COMP) for values in basis
     ]
-    for copy in copies:
-        copy.start()
+    sub = row_of((8, SEC * COMP))
+    parts = []
+    for places in (
+        range(20),
+        range(4, 24),
+        [8 * b + i for b in range(4) for i in range(5)],
+    ):
+        tiles = {}
+        for place, row in zip(places, rows):
+            tile = tiles.get(place // 8, jnp.zeros((8, SEC * COMP), jnp.float32))
+            tiles[place // 8] = jnp.where(sub == place % 8, row, tile)
+        rest = jnp.concatenate([tiles[i] for i in sorted(tiles)])
+        for _ in range(3):
+            part = rest.astype(jnp.bfloat16).astype(jnp.float32)
+            parts.append(part)
+            rest = rest - part
+    return jnp.concatenate(parts).astype(jnp.bfloat16)
+
+
+TAIL = 8
+ORDER = ((TAIL, 0, 1, 2, 3, 4, 5, 6, 7),)
+
+
+def project_kernel(strain_hbm, send_ref, energy_ref, buf, a_ref, sem):
+    copies = {}
+    for group in ORDER:
+        for u in group:
+            for l in range(4 * u, 4 * u + 4):
+                copies[l] = pltpu.make_async_copy(strain_hbm.at[:, l], buf.at[l], sem.at[l])
+                copies[l].start()
     rows = buf.reshape(LAY, SEC * COMP, LANES)
     tops = {}
     sums = {}
+    tails = {}
     sub = row_of((8, LANES))
     block = lane_of((8, LANES)) // 32
 
@@ -141,56 +135,61 @@
         d = d[:size] + d[size : 2 * size] + d[2 * size :]
         for i in range(2):
             l = 2 * t + i
-            slot = l % CHUNK
-            wide = rows[l].astype(jnp.float32)
-            squares[slot] = wide * wide
-            e = squares[slot, pl.ds(0, SEC, stride=2), :] + squares[slot, pl.ds(1, SEC, stride=2), :]
+            c0 = rows[l, pl.ds(0, SEC, stride=2), :].astype(jnp.float32)
+            c1 = rows[l, pl.ds(1, SEC, stride=2), :].astype(jnp.float32)
+            e = c0 * c0 + c1 * c1
             energy_ref[l] = e
             tops[l] = jnp.max(e, axis=0, keepdims=True)
             sums[l] = d[:, LANES * i : LANES * (i + 1)]
 
-    for l in range(LAY):
-        if l % CHUNK == 0:
-            for other in range(l, min(l + CHUNK, LAY)):
-                copies[other].wait()
-        if l % 2 == 0:
-            pair(l // 2)
-
-    tails = {}
-    for v in range(4):
-        x = sums[32 + v]
-        shifted = []
-        for delta in range(4):
-            w = jnp.zeros((8, LANES), jnp.float32)
-            for b in range(4):
-                w = jnp.where(block == (b - delta) % 4, x[8 * b : 8 * b + 8], w)
-            shifted.append(pltpu.roll(w, 32 * delta, 1) if delta else w)
-        for g in range(4):
-            y = shifted[0]
-            for b in range(4):
-                y = jnp.where(block == b, shifted[(b - g) % 4], y)
-            tails[v, g] = y
-
-    for u in range(8):
+    def pack_tail():
+        for v in range(4):
+            x = sums[32 + v]
+            shifted = []
+            for delta in range(4):
+                w = jnp.zeros((8, LANES), jnp.float32)
+                for b in range(4):
+                    w = jnp.where(block == (b - delta) % 4, x[8 * b : 8 * b + 8], w)
+                shifted.append(pltpu.roll(w, 32 * delta, 1) if delta else w)
+            for g in range(4):
+                y = shifted[0]
+                for b in range(4):
+                    y = jnp.where(block == b, shifted[(b - g) % 4], y)
+                top = tops[32 + v]
+                if g:
+                    top = pltpu.roll(top, LANES - 32 * g, 1)
+                tails[v, g] = jnp.where(sub == 7, top, y)
+
+    def pack(u):
         first = halves(sums[4 * u], sums[4 * u + 1])
         second = halves(sums[4 * u + 2], sums[4 * u + 3])
         top0 = halves(tops[4 * u], tops[4 * u + 1])
         top1 = halves(tops[4 * u + 2], tops[4 * u + 3])
         for h in range(2):
             c = 2 * u + h
-            v, g = u // 2, quarter_of(u, h)
             send_ref[c, 0:16] = first[h][0:16]
             send_ref[c, 16:24] = first[h][16:24] + second[h][0:8]
             send_ref[c, 24:40] = second[h][8:24]
-            top2 = tops[32 + v]
-            if g:
-                top2 = pltpu.roll(top2, LANES - 32 * g, 1)
-            tile = jnp.where(sub == 5, top0[h], tails[v, g])
-            tile = jnp.where(sub == 6, top1[h], tile)
-            send_ref[c, 40:48] = jnp.where(sub == 7, top2, tile)
-
-
-def project(strain, a):
+            tile = jnp.where(sub == 5, top0[h], tails[u // 2, quarter_of(u, h)])
+            send_ref[c, 40:48] = jnp.where(sub == 6, top1[h], tile)
+
+    a_ref[...] = window_matrix()
+    waiting = []
+    for group in ORDER:
+        for u in group:
+            for l in range(4 * u, 4 * u + 4):
+                copies[l].wait()
+        for u in group:
+            pair(2 * u)
+            pair(2 * u + 1)
+        for u in waiting:
+            pack_tail() if u == TAIL else pack(u)
+        waiting = group
+    for u in waiting:
+        pack_tail() if u == TAIL else pack(u)
+
+
+def project(strain):
     return pl.pallas_call(
         project_kernel,
         name="project",
@@ -198,15 +197,15 @@
             jax.ShapeDtypeStruct((CIRC, ROWS, LANES), jnp.float32),
             jax.ShapeDtypeStruct((LAY, SEC, LANES), jnp.float32),
         ],
-        in_specs=[pl.BlockSpec(memory_space=pl.ANY), pl.BlockSpec(memory_space=pltpu.VMEM)],
+        in_specs=[pl.BlockSpec(memory_space=pl.ANY)],
         out_specs=[pl.BlockSpec(memory_space=pltpu.VMEM)] * 2,
         scratch_shapes=[
             pltpu.VMEM((LAY, SEC, COMP, LANES), jnp.bfloat16),
-            pltpu.VMEM((CHUNK, SEC * COMP, LANES), jnp.float32),
+            pltpu.VMEM((240, SEC * COMP), jnp.bfloat16),
             pltpu.SemaphoreType.DMA((LAY,)),
         ],
-        compiler_params=pltpu.CompilerParams(vmem_limit_bytes=32 * 2**20),
-    )(strain, a)
+        compiler_params=pltpu.CompilerParams(vmem_limit_bytes=50 * 2**20),
+    )(strain)
 
 
 def owner_kernel(
@@ -434,8 +433,8 @@
     )(everything, energy, region, temp, cond, stiff)
 
 
-def per_device(sects, a, w, strain, region, prior, temp, cond, loss, mullins, stiff):
-    send, energy = project(strain.transpose(0, 2, 1, 3), a)
+def per_device(sects, w, strain, region, prior, temp, cond, loss, mullins, stiff):
+    send, energy = project(strain.transpose(0, 2, 1, 3))
     recv = lax.all_to_all(send, "circ", 0, 0, tiled=True)
     own, msg = owner(
         recv.reshape(CIRC * ROWS, LANES), w, region, prior, temp, cond, loss, mullins.reshape(1, NREG)
@@ -455,13 +454,12 @@
 
 
 def solution(mesh):
-    a = project_matrix()
     w = combine_matrix()
     maps = P(None, "sect")
 
     def whole(*args):
         return jax.shard_map(
-            functools.partial(per_device, mesh.shape["sect"], jnp.asarray(a), jnp.asarray(w)),
+            functools.partial(per_device, mesh.shape["sect"], jnp.asarray(w)),
             mesh=mesh,
             in_specs=(P("circ", None, None, "sect"), maps, maps, maps, maps, P(), P(), P()),
             out_specs=(maps, maps, P("circ", None, "sect")),

time: 59.4 us -> 54.7 us (0.921)
  local copies, waits for them, and re-layouts: 2.61 us -> 0.05 us
  Pallas kernels: 9.02 us -> 6.8 us
    unnamed x20 -> x16, local copies, waits for them, and re-layouts: 2.6 us -> 0.04 us
    pallas_call x1, Pallas kernels: 6.52 us -> 4.3 us  [project(): pl.pallas_call(project_kernel, name='project', out_shape=[jax.ShapeDtypeS...]
where the time goes in v2:
time: 54.7 us; the launch traced here: 54.4 us
  blocking collectives  38.9 us (71%)
  Pallas kernels  6.8 us (12%)
  waiting for transfers between devices  6.01 us (11%)
  starting transfers between devices  1.91 us (3%)
  between operations  0.75 us (1%)
    all_to_all x1, blocking collectives, per_device(): recv = lax.all_to_all(send, 'circ', 0, 0, tiled=True)  24.4 us
    all_to_all x1, blocking collectives, per_device(): everything = lax.all_to_all(block, 'circ', 0, 0, tiled=True)  14.5 us
    ppermute x1, waiting for transfers between devices, per_device(): halo = lax.ppermute(msg, ('circ', 'sect'), pairs)  6.01 us
    pallas_call x1, Pallas kernels, project(): pl.pallas_call(project_kernel, name='project', out_shape=[jax.ShapeDtypeS...  4.3 us
    pallas_call x1, Pallas kernels, soften(): pl.pallas_call(modulus_kernel, name='modulus', out_shape=[jax.ShapeDtypeS...  1.98 us
    ppermute x1, starting transfers between devices, per_device(): halo = lax.ppermute(msg, ('circ', 'sect'), pairs)  1.91 us
  transfers between devices with their start and end apart: 1, of which 1 were waited for; matrix products, arithmetic and copies ran while one was open for 0% of the time, Pallas kernels for 0%

profile of v2, /device:TPU:256, one launch (start us, length us, event | category | flops | bytes accessed | tf_op | source)
XLA Modules:
  0.0 54.4 jit_solution(16831329781872618213)
XLA Ops:
  0.6 0.0 copy-start
  0.6 0.0 copy-start.3
  0.7 0.0 copy-start.2
  0.7 0.0 copy-start.1
  0.7 0.0 copy-start.6
  0.7 0.0 copy-start.5
  0.7 0.0 copy-start.4
  0.7 0.0 copy-start.7
  0.7 4.3 %project.1 = (f32[16,48,128]{2,1,0:T(8,128)S(1)}, f32[36,128,128]{2,1,0:T(8,128)S(1)}) custom-call(bf16[128,36,2,128]{3,2,1,0:T(2,128)(2,1)} %bitcast.10), custom_call_target="tpu_custom_call" | custom-call | tf_op jit(solution)/shard_map/project/pallas_call | solution.py:193
  5.0 24.4 %all_to_all.10 = f32[16,48,128]{2,1,0:T(8,128)S(1)} all-to-all(f32[16,48,128]{2,1,0:T(8,128)S(1)} %get-tuple-element.10), channel_id=1, replica_groups=mesh['circ'=16,'sect'=32] {'circ'}, dimensions={0} | all-to-all | bytes 786432 | tf_op jit(solution)/shard_map/all_to_all | solution.py:438
  29.4 0.0 copy-done
  29.4 0.0 copy-done.3
  29.4 0.0 copy-done.2
  29.4 0.0 copy-done.1
  29.4 0.0 copy-done.6
  29.5 0.0 copy-done.5
  29.5 0.0 copy-done.4
  29.5 0.5 owner.1
  30.0 1.9 %collective-permute-start = (f32[8,128]{1,0:T(8,128)S(1)}, f32[8,128]{1,0:T(8,128)S(1)}, u32[]{:S(2)}, u32[]{:S(2)}) collective-permute-start(f32[8,128]{1,0:T(8,128)S(1)} %get-tuple-element.12), channel_id=1, source_target_pairs={{1,32},{32,1},{65,96},{96,65},{129,160},{160,129},{193,224},{224,1... | collective-permute-start | bytes 12296 | tf_op jit(solution)/shard_map/ppermute | solution.py:447
  31.9 6.0 %collective-permute-done = f32[8,128]{1,0:T(8,128)S(1)} collective-permute-done((f32[8,128]{1,0:T(8,128)S(1)}, f32[8,128]{1,0:T(8,128)S(1)}, u32[]{:S(2)}, u32[]{:S(2)}) %collective-permute-start) | collective-permute-done | bytes 4128 | tf_op jit(solution)/shard_map/ppermute | solution.py:447
  37.9 14.5 %all_to_all.11 = f32[16,8,128]{2,1,0:T(8,128)S(1)} all-to-all(f32[16,8,128]{2,1,0:T(8,128)S(1)} %broadcast_in_dim.2), channel_id=1, replica_groups=mesh['circ'=16,'sect'=32] {'circ'}, dimensions={0} | all-to-all | bytes 131072 | tf_op jit(solution)/shard_map/all_to_all | solution.py:449
  52.4 0.0 copy-done.7
  52.4 2.0 %modulus.1 = (f32[36,128]{1,0:T(8,128)}, f32[36,128]{1,0:T(8,128)}, bf16[36,128,128]{2,1,0:T(8,128)(2,1)}) custom-call(f32[128,128]{1,0:T(8,128)S(1)} %bitcast.7, f32[36,128,128]{2,1,0:T(8,128)S(1)} %get-tuple-element.13.energy_ref, s32[36,128]{1,0:T(8,128)S(1)} %copy-done.1, f32[36,128]{1,0:T(8,128)S(1)} %copy-done.2, f32[36,128]{1,0:T(8,128)S(1)} %copy-done.3, ...), custom_call_target="tpu_custom_call" | custom-call | tf_op jit(solution)/shard_map/modulus/pallas_call | solution.py:415
  (2 shorter events, 0.0 us)
Async XLA Ops:
  0.6 28.8 %copy-start = (bf16[256,768]{1,0:T(8,128)(2,1)S(1)}, bf16[256,768]{1,0:T(8,128)(2,1)}, u32[]{:S(2)}) copy-start(bf16[256,768]{1,0:T(8,128)(2,1)} %constant.2.clone.w_ref) | copy-start | bytes 1179652
  0.6 28.8 %copy-start.3 = (f32[36,128]{1,0:T(8,128)S(1)}, f32[36,128]{1,0:T(8,128)}, u32[]{:S(2)}) copy-start(f32[36,128]{1,0:T(8,128)} %cond_ref.3) | copy-start | bytes 55300
  0.7 28.8 %copy-start.2 = (f32[36,128]{1,0:T(8,128)S(1)}, f32[36,128]{1,0:T(8,128)}, u32[]{:S(2)}) copy-start(f32[36,128]{1,0:T(8,128)} %temp_ref.3) | copy-start | bytes 55300
  0.7 28.8 %copy-start.1 = (s32[36,128]{1,0:T(8,128)S(1)}, s32[36,128]{1,0:T(8,128)}, u32[]{:S(2)}) copy-start(s32[36,128]{1,0:T(8,128)} %region_ref.3) | copy-start | bytes 55300
  0.7 28.8 %copy-start.6 = (f32[8]{0:T(128)S(1)}, f32[8]{0:T(128)}, u32[]{:S(2)}) copy-start(f32[8]{0:T(128)} %param.15) | copy-start | bytes 100
  0.7 28.8 %copy-start.5 = (f32[8,8]{1,0:T(8,128)S(1)}, f32[8,8]{1,0:T(8,128)}, u32[]{:S(2)}) copy-start(f32[8,8]{1,0:T(8,128)} %loss_ref.1) | copy-start | bytes 772
  0.7 28.8 %copy-start.4 = (f32[36,128]{1,0:T(8,128)S(1)}, f32[36,128]{1,0:T(8,128)}, u32[]{:S(2)}) copy-start(f32[36,128]{1,0:T(8,128)} %prior_ref.1) | copy-start | bytes 55300
  0.7 51.7 %copy-start.7 = (f32[8]{0:T(128)S(1)}, f32[8]{0:T(128)}, u32[]{:S(2)}) copy-start(f32[8]{0:T(128)} %param.16) | copy-start | bytes 100
  30.0 7.9 %collective-permute-start = (f32[8,128]{1,0:T(8,128)S(1)}, f32[8,128]{1,0:T(8,128)S(1)}, u32[]{:S(2)}, u32[]{:S(2)}) collective-permute-start(f32[8,128]{1,0:T(8,128)S(1)} %get-tuple-element.12), channel_id=1, source_target_pairs={{1,32},{32,1},{65,96},{96,65},{129,160},{160,129},{193,224},{224,1... | collective-permute-start | bytes 12296 | tf_op jit(solution)/shard_map/ppermute | solution.py:447

commit v3 on v2

--- a/solution.py
+++ b/solution.py
@@ -82,12 +82,12 @@
 def window_matrix():
     wide = (1, SEC * COMP)
     lane = lane_of(wide)
-    t = ((lane // 2).astype(jnp.float32) - 0.5 * (SEC - 1)) * (2.0 / (SEC - 1))
+    t = ((lane % SEC).astype(jnp.float32) - 0.5 * (SEC - 1)) * (2.0 / (SEC - 1))
     basis = [jnp.ones(wide, jnp.float32), t]
     for _ in range(RANK - 2):
         basis.append(2.0 * t * basis[-1] - basis[-2])
     rows = [
-        jnp.where(lane % 2 == comp, values, 0.0) for comp in range(COMP) for values in basis
+        jnp.where(lane // SEC == comp, values, 0.0) for comp in range(COMP) for values in basis
     ]
     sub = row_of((8, SEC * COMP))
     parts = []
@@ -109,7 +109,7 @@
 
 
 TAIL = 8
-ORDER = ((TAIL, 0, 1, 2, 3, 4, 5, 6, 7),)
+ORDER = ((TAIL, 0, 1), (2, 3, 4), (5, 6, 7))
 
 
 def project_kernel(strain_hbm, send_ref, energy_ref, buf, a_ref, sem):
@@ -120,6 +120,7 @@
                 copies[l] = pltpu.make_async_copy(strain_hbm.at[:, l], buf.at[l], sem.at[l])
                 copies[l].start()
     rows = buf.reshape(LAY, SEC * COMP, LANES)
+    parity = lax.axis_index("sect") % 2
     tops = {}
     sums = {}
     tails = {}
@@ -130,13 +131,14 @@
         kind = 2 if t >= 16 else t % 2
         size = 32 if kind == 2 else 24
         base = 72 * kind
-        x = jnp.concatenate([rows[2 * t], rows[2 * t + 1]], axis=1)
-        d = jnp.dot(a_ref[base : base + 3 * size], x, preferred_element_type=jnp.float32)
+        x = [[rows[2 * t + i, pl.ds(c, SEC, stride=COMP), :] for i in range(2)] for c in range(COMP)]
+        wide = jnp.concatenate([jnp.concatenate(both, axis=1) for both in x])
+        d = jnp.dot(a_ref[base : base + 3 * size], wide, preferred_element_type=jnp.float32)
         d = d[:size] + d[size : 2 * size] + d[2 * size :]
         for i in range(2):
             l = 2 * t + i
-            c0 = rows[l, pl.ds(0, SEC, stride=2), :].astype(jnp.float32)
-            c1 = rows[l, pl.ds(1, SEC, stride=2), :].astype(jnp.float32)
+            c0 = x[0][i].astype(jnp.float32)
+            c1 = x[1][i].astype(jnp.float32)
             e = c0 * c0 + c1 * c1
             energy_ref[l] = e
             tops[l] = jnp.max(e, axis=0, keepdims=True)
@@ -166,7 +168,7 @@
         top0 = halves(tops[4 * u], tops[4 * u + 1])
         top1 = halves(tops[4 * u + 2], tops[4 * u + 3])
         for h in range(2):
-            c = 2 * u + h
+            c = 2 * u + (h + parity) % 2
             send_ref[c, 0:16] = first[h][0:16]
             send_ref[c, 16:24] = first[h][16:24] + second[h][0:8]
             send_ref[c, 24:40] = second[h][8:24]
@@ -213,7 +215,7 @@
 ):
     c = lax.axis_index("circ")
     u = c // 2
-    h = c % 2
+    h = (c + lax.axis_index("sect")) % 2
     is_left = h == 0
     lane = lane_of((1, LANES))
     sub = row_of((8, LANES))
@@ -324,6 +326,8 @@
 ):
     low = lane_of((8, LANES)) < 64
     lane = lane_of((FIELD_ROWS, LANES))
+    parity = lax.axis_index("sect") % 2
+    at = [8 * parity, 8 * (1 - parity)]
     for scratch in (heat_s, peak_s, halo_s, cond_s, temp_s):
         scratch[32:FIELD_ROWS] = jnp.zeros((8, LANES), jnp.float32)
     region_s[32:FIELD_ROWS] = jnp.zeros((8, LANES), jnp.int32)
@@ -332,15 +336,15 @@
     region_s[0:LAY] = region_ref[...]
     for a in range(2):
         for base, target in ((0, heat_s), (2, peak_s)):
-            left = all_ref[pl.ds(base + a, 8, stride=16), :]
-            right = all_ref[pl.ds(8 + base + a, 8, stride=16), :]
+            left = all_ref[pl.ds(at[0] + base + a, 8, stride=16), :]
+            right = all_ref[pl.ds(at[1] + base + a, 8, stride=16), :]
             target[pl.ds(2 * a, 8, stride=4), :] = jnp.where(low, left, pltpu.roll(right, 64, 1))
             target[pl.ds(2 * a + 1, 8, stride=4), :] = jnp.where(low, pltpu.roll(left, 64, 1), right)
     small = lane_of((4, LANES))
     for base, target in ((4, heat_s), (5, peak_s)):
         row = jnp.zeros((4, LANES), jnp.float32)
         for odd, h, g in ((0, 0, 0), (1, 0, 1), (1, 1, 2), (0, 1, 3)):
-            part = all_ref[pl.ds(16 * odd + 8 * h + base, 4, stride=32), :]
+            part = all_ref[pl.ds(at[h] + 16 * odd + base, 4, stride=32), :]
             if g != 1:
                 part = pltpu.roll(part, (32 * g - 32) % LANES, 1)
             row = jnp.where(small // 32 == g, part, row)
@@ -350,8 +354,10 @@
     for j in range(4):
         both = all_ref[pl.ds(4 + j, 8, stride=16), :] + all_ref[pl.ds(12 + j, 8, stride=16), :]
         halo_s[pl.ds(j, 8, stride=4), :] = jnp.where(outer, both, 0.0)
-    from_left = pltpu.roll(all_ref[pl.ds(6, 4, stride=32), :], 32, 1)
-    from_right = pltpu.roll(all_ref[pl.ds(14, 4, stride=32), :], 96, 1)
+    from_left = all_ref[pl.ds(at[0] + 6, 4, stride=32), :]
+    from_right = all_ref[pl.ds(at[1] + 6, 4, stride=32), :]
+    from_left = pltpu.roll(from_left, 32, 1)
+    from_right = pltpu.roll(from_right, 96, 1)
     halo_s[32:LAY] = jnp.where(
         small >= LANES - 3 * EDGE, from_left, jnp.where(small < 3 * EDGE, from_right, 0.0)
     )
@@ -441,9 +447,9 @@
     )
     pairs = []
     for s in range(1, sects):
-        for u in range(CIRC // 2):
-            left, right = 2 * u * sects + s, (2 * u + 1) * sects + s - 1
-            pairs += [(left, right), (right, left)]
+        for c in range(s % 2, CIRC, 2):
+            here = c * sects + s
+            pairs += [(here, here - 1), (here - 1, here)]
     halo = lax.ppermute(msg, ("circ", "sect"), pairs)
     block = jnp.broadcast_to((own + halo)[None], (CIRC, 8, LANES))
     everything = lax.all_to_all(block, "circ", 0, 0, tiled=True)

time: 54.7 us -> 52.3 us (0.956)
  Pallas kernels: 6.8 us -> 5.3 us
  waiting for transfers between devices: 6.01 us -> 5.11 us
    pallas_call x1, Pallas kernels: 4.3 us -> 2.87 us  [project(): pl.pallas_call(project_kernel, name='project', out_shape=[jax.ShapeDtypeS...]
    ppermute x1, waiting for transfers between devices: 6.01 us -> 5.11 us  [per_device(): halo = lax.ppermute(msg, ('circ', 'sect'), pairs)]
where the time goes in v3:
time: 52.3 us; the launch traced here: 52.1 us
  blocking collectives  38.9 us (74%)
  Pallas kernels  5.3 us (10%)
  waiting for transfers between devices  5.11 us (10%)
  starting transfers between devices  1.91 us (4%)
  between operations  0.75 us (1%)
    all_to_all x1, blocking collectives, per_device(): recv = lax.all_to_all(send, 'circ', 0, 0, tiled=True)  24.4 us
    all_to_all x1, blocking collectives, per_device(): everything = lax.all_to_all(block, 'circ', 0, 0, tiled=True)  14.5 us
    ppermute x1, waiting for transfers between devices, per_device(): halo = lax.ppermute(msg, ('circ', 'sect'), pairs)  5.11 us
    pallas_call x1, Pallas kernels, project(): pl.pallas_call(project_kernel, name='project', out_shape=[jax.ShapeDtypeS...  2.87 us
    pallas_call x1, Pallas kernels, soften(): pl.pallas_call(modulus_kernel, name='modulus', out_shape=[jax.ShapeDtypeS...  1.92 us
    ppermute x1, starting transfers between devices, per_device(): halo = lax.ppermute(msg, ('circ', 'sect'), pairs)  1.91 us
  transfers between devices with their start and end apart: 1, of which 1 were waited for; matrix products, arithmetic and copies ran while one was open for 0% of the time, Pallas kernels for 0%

profile of v3, /device:TPU:256, one launch (start us, length us, event | category | flops | bytes accessed | tf_op | source)
XLA Modules:
  0.0 52.1 jit_solution(14569217851118861694)
XLA Ops:
  0.6 0.0 copy-start
  0.6 0.0 copy-start.3
  0.7 0.0 copy-start.2
  0.7 0.0 copy-start.1
  0.7 0.0 copy-start.6
  0.7 0.0 copy-start.5
  0.7 0.0 copy-start.4
  0.7 0.0 copy-start.7
  0.7 2.9 %project.1 = (f32[16,48,128]{2,1,0:T(8,128)S(1)}, f32[36,128,128]{2,1,0:T(8,128)S(1)}) custom-call(bf16[128,36,2,128]{3,2,1,0:T(2,128)(2,1)} %bitcast.10), custom_call_target="tpu_custom_call" | custom-call | tf_op jit(solution)/shard_map/project/pallas_call | solution.py:195
  3.6 24.4 %all_to_all.10 = f32[16,48,128]{2,1,0:T(8,128)S(1)} all-to-all(f32[16,48,128]{2,1,0:T(8,128)S(1)} %get-tuple-element.10), channel_id=1, replica_groups=mesh['circ'=16,'sect'=32] {'circ'}, dimensions={0} | all-to-all | bytes 786432 | tf_op jit(solution)/shard_map/all_to_all | solution.py:444
  28.0 0.0 copy-done
  28.0 0.0 copy-done.3
  28.0 0.0 copy-done.2
  28.0 0.0 copy-done.1
  28.0 0.0 copy-done.6
  28.0 0.0 copy-done.5
  28.0 0.0 copy-done.4
  28.0 0.5 owner.1
  28.6 1.9 %collective-permute-start = (f32[8,128]{1,0:T(8,128)S(1)}, f32[8,128]{1,0:T(8,128)S(1)}, u32[]{:S(2)}, u32[]{:S(2)}) collective-permute-start(f32[8,128]{1,0:T(8,128)S(1)} %get-tuple-element.12), channel_id=1, source_target_pairs={{33,32},{32,33},{97,96},{96,97},{161,160},{160,161},{225,224},{224... | collective-permute-start | bytes 12296 | tf_op jit(solution)/shard_map/ppermute | solution.py:453
  30.5 5.1 %collective-permute-done = f32[8,128]{1,0:T(8,128)S(1)} collective-permute-done((f32[8,128]{1,0:T(8,128)S(1)}, f32[8,128]{1,0:T(8,128)S(1)}, u32[]{:S(2)}, u32[]{:S(2)}) %collective-permute-start) | collective-permute-done | bytes 4128 | tf_op jit(solution)/shard_map/ppermute | solution.py:453
  35.6 14.5 %all_to_all.11 = f32[16,8,128]{2,1,0:T(8,128)S(1)} all-to-all(f32[16,8,128]{2,1,0:T(8,128)S(1)} %broadcast_in_dim.2), channel_id=1, replica_groups=mesh['circ'=16,'sect'=32] {'circ'}, dimensions={0} | all-to-all | bytes 131072 | tf_op jit(solution)/shard_map/all_to_all | solution.py:455
  50.1 0.0 copy-done.7
  50.1 1.9 %modulus.1 = (f32[36,128]{1,0:T(8,128)}, f32[36,128]{1,0:T(8,128)}, bf16[36,128,128]{2,1,0:T(8,128)(2,1)}) custom-call(f32[128,128]{1,0:T(8,128)S(1)} %bitcast.7, f32[36,128,128]{2,1,0:T(8,128)S(1)} %get-tuple-element.13.energy_ref, s32[36,128]{1,0:T(8,128)S(1)} %copy-done.1, f32[36,128]{1,0:T(8,128)S(1)} %copy-done.2, f32[36,128]{1,0:T(8,128)S(1)} %copy-done.3, ...), custom_call_target="tpu_custom_call" | custom-call | tf_op jit(solution)/shard_map/modulus/pallas_call | solution.py:421
  (2 shorter events, 0.0 us)
Async XLA Ops:
  0.6 27.4 %copy-start = (bf16[256,768]{1,0:T(8,128)(2,1)S(1)}, bf16[256,768]{1,0:T(8,128)(2,1)}, u32[]{:S(2)}) copy-start(bf16[256,768]{1,0:T(8,128)(2,1)} %constant.2.clone.w_ref) | copy-start | bytes 1179652
  0.6 27.4 %copy-start.3 = (f32[36,128]{1,0:T(8,128)S(1)}, f32[36,128]{1,0:T(8,128)}, u32[]{:S(2)}) copy-start(f32[36,128]{1,0:T(8,128)} %cond_ref.3) | copy-start | bytes 55300
  0.7 27.3 %copy-start.2 = (f32[36,128]{1,0:T(8,128)S(1)}, f32[36,128]{1,0:T(8,128)}, u32[]{:S(2)}) copy-start(f32[36,128]{1,0:T(8,128)} %temp_ref.3) | copy-start | bytes 55300
  0.7 27.3 %copy-start.1 = (s32[36,128]{1,0:T(8,128)S(1)}, s32[36,128]{1,0:T(8,128)}, u32[]{:S(2)}) copy-start(s32[36,128]{1,0:T(8,128)} %region_ref.3) | copy-start | bytes 55300
  0.7 27.3 %copy-start.6 = (f32[8]{0:T(128)S(1)}, f32[8]{0:T(128)}, u32[]{:S(2)}) copy-start(f32[8]{0:T(128)} %param.15) | copy-start | bytes 100
  0.7 27.3 %copy-start.5 = (f32[8,8]{1,0:T(8,128)S(1)}, f32[8,8]{1,0:T(8,128)}, u32[]{:S(2)}) copy-start(f32[8,8]{1,0:T(8,128)} %loss_ref.1) | copy-start | bytes 772
  0.7 27.3 %copy-start.4 = (f32[36,128]{1,0:T(8,128)S(1)}, f32[36,128]{1,0:T(8,128)}, u32[]{:S(2)}) copy-start(f32[36,128]{1,0:T(8,128)} %prior_ref.1) | copy-start | bytes 55300
  0.7 49.4 %copy-start.7 = (f32[8]{0:T(128)S(1)}, f32[8]{0:T(128)}, u32[]{:S(2)}) copy-start(f32[8]{0:T(128)} %param.16) | copy-start | bytes 100
  28.6 7.0 %collective-permute-start = (f32[8,128]{1,0:T(8,128)S(1)}, f32[8,128]{1,0:T(8,128)S(1)}, u32[]{:S(2)}, u32[]{:S(2)}) collective-permute-start(f32[8,128]{1,0:T(8,128)S(1)} %get-tuple-element.12), channel_id=1, source_target_pairs={{33,32},{32,33},{97,96},{96,97},{161,160},{160,161},{225,224},{224... | collective-permute-start | bytes 12296 | tf_op jit(solution)/shard_map/ppermute | solution.py:453

commit v4 on v3

--- a/solution.py
+++ b/solution.py
@@ -116,10 +116,11 @@
     copies = {}
     for group in ORDER:
         for u in group:
-            for l in range(4 * u, 4 * u + 4):
-                copies[l] = pltpu.make_async_copy(strain_hbm.at[:, l], buf.at[l], sem.at[l])
-                copies[l].start()
-    rows = buf.reshape(LAY, SEC * COMP, LANES)
+            copies[u] = pltpu.make_async_copy(
+                strain_hbm.at[:, pl.ds(4 * u, 4)], buf.at[u], sem.at[u]
+            )
+            copies[u].start()
+    rows = buf.reshape(LAY // 4, SEC * 4 * COMP, LANES)
     parity = lax.axis_index("sect") % 2
     tops = {}
     sums = {}
@@ -131,7 +132,11 @@
         kind = 2 if t >= 16 else t % 2
         size = 32 if kind == 2 else 24
         base = 72 * kind
-        x = [[rows[2 * t + i, pl.ds(c, SEC, stride=COMP), :] for i in range(2)] for c in range(COMP)]
+        first = 4 * (t % 2)
+        x = [
+            [rows[t // 2, pl.ds(first + COMP * i + c, SEC, stride=4 * COMP), :] for i in range(2)]
+            for c in range(COMP)
+        ]
         wide = jnp.concatenate([jnp.concatenate(both, axis=1) for both in x])
         d = jnp.dot(a_ref[base : base + 3 * size], wide, preferred_element_type=jnp.float32)
         d = d[:size] + d[size : 2 * size] + d[2 * size :]
@@ -179,8 +184,7 @@
     waiting = []
     for group in ORDER:
         for u in group:
-            for l in range(4 * u, 4 * u + 4):
-                copies[l].wait()
+            copies[u].wait()
         for u in group:
             pair(2 * u)
             pair(2 * u + 1)
@@ -202,9 +206,9 @@
         in_specs=[pl.BlockSpec(memory_space=pl.ANY)],
         out_specs=[pl.BlockSpec(memory_space=pltpu.VMEM)] * 2,
         scratch_shapes=[
-            pltpu.VMEM((LAY, SEC, COMP, LANES), jnp.bfloat16),
+            pltpu.VMEM((LAY // 4, SEC, 4, COMP, LANES), jnp.bfloat16),
             pltpu.VMEM((240, SEC * COMP), jnp.bfloat16),
-            pltpu.SemaphoreType.DMA((LAY,)),
+            pltpu.SemaphoreType.DMA((LAY // 4,)),
         ],
         compiler_params=pltpu.CompilerParams(vmem_limit_bytes=50 * 2**20),
     )(strain)
@@ -317,12 +321,13 @@
 
 
 GROUPS = 6
+EARLY = 12
 
 
 def modulus_kernel(
     all_ref, energy_ref, region_ref, temp_ref, cond_ref, stiff_ref,
     field_hbm, peak_hbm, out_hbm,
-    heat_s, peak_s, halo_s, cond_s, temp_s, region_s, field_s, out_s, sem,
+    heat_s, peak_s, halo_s, cond_s, temp_s, region_s, field_s, soft_s, out_s, sem,
 ):
     low = lane_of((8, LANES)) < 64
     lane = lane_of((FIELD_ROWS, LANES))
@@ -362,6 +367,7 @@
         small >= LANES - 3 * EDGE, from_left, jnp.where(small < 3 * EDGE, from_right, 0.0)
     )
 
+    peak = peak_s[...]
     halo = halo_s[...]
 
     def unpack(n):
@@ -371,7 +377,6 @@
             lane < EDGE, low_part, jnp.where(lane >= LANES - EDGE, high_part, 0.0)
         )
 
-    peak = peak_s[...]
     heat = (heat_s[...], unpack(0))
     cond = (cond_s[...], unpack(1))
     field = (temp_s[...], unpack(2))
@@ -390,6 +395,8 @@
             beside = beside + pltpu.roll(field[i], 1, 0) + pltpu.roll(field[i], FIELD_ROWS - 1, 0)
             new.append(jnp.where(valid, heat[i] + cond[i] * beside, 0.0))
         field = new
+    for l in range(EARLY):
+        soft_s[l] = 1.0 - 0.5 * jnp.tanh((peak[l : l + 1] - energy_ref[l]) * 0.25)
     field_s[...] = field[0]
     copies = [
         pltpu.make_async_copy(field_s.at[0:LAY], field_hbm, sem.at[0]),
@@ -405,8 +412,11 @@
     size = LAY // GROUPS
     for group in range(GROUPS):
         for l in range(group * size, (group + 1) * size):
-            soft = jnp.tanh((peak[l : l + 1] - energy_ref[l]) * 0.25)
-            out_s[l] = (factor[l : l + 1] * (1.0 - 0.5 * soft)).astype(jnp.bfloat16)
+            if l < EARLY:
+                soft = soft_s[l]
+            else:
+                soft = 1.0 - 0.5 * jnp.tanh((peak[l : l + 1] - energy_ref[l]) * 0.25)
+            out_s[l] = (factor[l : l + 1] * soft).astype(jnp.bfloat16)
         where = pl.ds(group * size, size)
         copy = pltpu.make_async_copy(out_s.at[where], out_hbm.at[where], sem.at[2 + group])
         copy.start()
@@ -432,6 +442,7 @@
             plane, plane, plane, plane, plane,
             pltpu.VMEM((FIELD_ROWS, LANES), jnp.int32),
             plane,
+            pltpu.VMEM((EARLY, SEC, LANES), jnp.float32),
             pltpu.VMEM((LAY, SEC, LANES), jnp.bfloat16),
             pltpu.SemaphoreType.DMA((2 + GROUPS,)),
         ],

time: 52.3 us -> 52.1 us (level)
  no operation moved by 1% of the time
where the time goes in v4:
time: 52.1 us; the launch traced here: 51.8 us
  blocking collectives  38.9 us (75%)
  waiting for transfers between devices  5.11 us (10%)
  Pallas kernels  5.09 us (10%)
  starting transfers between devices  1.91 us (4%)
  between operations  0.75 us (1%)
    all_to_all x1, blocking collectives, per_device(): recv = lax.all_to_all(send, 'circ', 0, 0, tiled=True)  24.4 us
    all_to_all x1, blocking collectives, per_device(): everything = lax.all_to_all(block, 'circ', 0, 0, tiled=True)  14.5 us
    ppermute x1, waiting for transfers between devices, per_device(): halo = lax.ppermute(msg, ('circ', 'sect'), pairs)  5.11 us
    pallas_call x1, Pallas kernels, project(): pl.pallas_call(project_kernel, name='project', out_shape=[jax.ShapeDtypeS...  2.65 us
    pallas_call x1, Pallas kernels, soften(): pl.pallas_call(modulus_kernel, name='modulus', out_shape=[jax.ShapeDtypeS...  1.92 us
    ppermute x1, starting transfers between devices, per_device(): halo = lax.ppermute(msg, ('circ', 'sect'), pairs)  1.91 us
  transfers between devices with their start and end apart: 1, of which 1 were waited for; matrix products, arithmetic and copies ran while one was open for 0% of the time, Pallas kernels for 0%

profile of v4, /device:TPU:256, one launch (start us, length us, event | category | flops | bytes accessed | tf_op | source)
XLA Modules:
  0.0 51.8 jit_solution(13981424460503273922)
XLA Ops:
  0.6 0.0 copy-start
  0.6 0.0 copy-start.3
  0.7 0.0 copy-start.2
  0.7 0.0 copy-start.1
  0.7 0.0 copy-start.6
  0.7 0.0 copy-start.5
  0.7 0.0 copy-start.4
  0.7 0.0 copy-start.7
  0.7 2.7 %project.1 = (f32[16,48,128]{2,1,0:T(8,128)S(1)}, f32[36,128,128]{2,1,0:T(8,128)S(1)}) custom-call(bf16[128,36,2,128]{3,2,1,0:T(2,128)(2,1)} %bitcast.10), custom_call_target="tpu_custom_call" | custom-call | tf_op jit(solution)/shard_map/project/pallas_call | solution.py:199
  3.4 24.4 %all_to_all.10 = f32[16,48,128]{2,1,0:T(8,128)S(1)} all-to-all(f32[16,48,128]{2,1,0:T(8,128)S(1)} %get-tuple-element.10), channel_id=1, replica_groups=mesh['circ'=16,'sect'=32] {'circ'}, dimensions={0} | all-to-all | bytes 786432 | tf_op jit(solution)/shard_map/all_to_all | solution.py:455
  27.8 0.0 copy-done
  27.8 0.0 copy-done.3
  27.8 0.0 copy-done.2
  27.8 0.0 copy-done.1
  27.8 0.0 copy-done.6
  27.8 0.0 copy-done.5
  27.8 0.0 copy-done.4
  27.8 0.5 owner.1
  28.3 1.9 %collective-permute-start = (f32[8,128]{1,0:T(8,128)S(1)}, f32[8,128]{1,0:T(8,128)S(1)}, u32[]{:S(2)}, u32[]{:S(2)}) collective-permute-start(f32[8,128]{1,0:T(8,128)S(1)} %get-tuple-element.12), channel_id=1, source_target_pairs={{33,32},{32,33},{97,96},{96,97},{161,160},{160,161},{225,224},{224... | collective-permute-start | bytes 12296 | tf_op jit(solution)/shard_map/ppermute | solution.py:464
  30.3 5.1 %collective-permute-done = f32[8,128]{1,0:T(8,128)S(1)} collective-permute-done((f32[8,128]{1,0:T(8,128)S(1)}, f32[8,128]{1,0:T(8,128)S(1)}, u32[]{:S(2)}, u32[]{:S(2)}) %collective-permute-start) | collective-permute-done | bytes 4128 | tf_op jit(solution)/shard_map/ppermute | solution.py:464
  35.4 14.5 %all_to_all.11 = f32[16,8,128]{2,1,0:T(8,128)S(1)} all-to-all(f32[16,8,128]{2,1,0:T(8,128)S(1)} %broadcast_in_dim.2), channel_id=1, replica_groups=mesh['circ'=16,'sect'=32] {'circ'}, dimensions={0} | all-to-all | bytes 131072 | tf_op jit(solution)/shard_map/all_to_all | solution.py:466
  49.9 0.0 copy-done.7
  49.9 1.9 %modulus.1 = (f32[36,128]{1,0:T(8,128)}, f32[36,128]{1,0:T(8,128)}, bf16[36,128,128]{2,1,0:T(8,128)(2,1)}) custom-call(f32[128,128]{1,0:T(8,128)S(1)} %bitcast.7, f32[36,128,128]{2,1,0:T(8,128)S(1)} %get-tuple-element.13.energy_ref, s32[36,128]{1,0:T(8,128)S(1)} %copy-done.1, f32[36,128]{1,0:T(8,128)S(1)} %copy-done.2, f32[36,128]{1,0:T(8,128)S(1)} %copy-done.3, ...), custom_call_target="tpu_custom_call" | custom-call | tf_op jit(solution)/shard_map/modulus/pallas_call | solution.py:431
  (2 shorter events, 0.0 us)
Async XLA Ops:
  0.6 27.1 %copy-start = (bf16[256,768]{1,0:T(8,128)(2,1)S(1)}, bf16[256,768]{1,0:T(8,128)(2,1)}, u32[]{:S(2)}) copy-start(bf16[256,768]{1,0:T(8,128)(2,1)} %constant.2.clone.w_ref) | copy-start | bytes 1179652
  0.6 27.1 %copy-start.3 = (f32[36,128]{1,0:T(8,128)S(1)}, f32[36,128]{1,0:T(8,128)}, u32[]{:S(2)}) copy-start(f32[36,128]{1,0:T(8,128)} %cond_ref.3) | copy-start | bytes 55300
  0.7 27.1 %copy-start.2 = (f32[36,128]{1,0:T(8,128)S(1)}, f32[36,128]{1,0:T(8,128)}, u32[]{:S(2)}) copy-start(f32[36,128]{1,0:T(8,128)} %temp_ref.3) | copy-start | bytes 55300
  0.7 27.1 %copy-start.1 = (s32[36,128]{1,0:T(8,128)S(1)}, s32[36,128]{1,0:T(8,128)}, u32[]{:S(2)}) copy-start(s32[36,128]{1,0:T(8,128)} %region_ref.3) | copy-start | bytes 55300
  0.7 27.1 %copy-start.6 = (f32[8]{0:T(128)S(1)}, f32[8]{0:T(128)}, u32[]{:S(2)}) copy-start(f32[8]{0:T(128)} %param.15) | copy-start | bytes 100
  0.7 27.1 %copy-start.5 = (f32[8,8]{1,0:T(8,128)S(1)}, f32[8,8]{1,0:T(8,128)}, u32[]{:S(2)}) copy-start(f32[8,8]{1,0:T(8,128)} %loss_ref.1) | copy-start | bytes 772
  0.7 27.1 %copy-start.4 = (f32[36,128]{1,0:T(8,128)S(1)}, f32[36,128]{1,0:T(8,128)}, u32[]{:S(2)}) copy-start(f32[36,128]{1,0:T(8,128)} %prior_ref.1) | copy-start | bytes 55300
  0.7 49.2 %copy-start.7 = (f32[8]{0:T(128)S(1)}, f32[8]{0:T(128)}, u32[]{:S(2)}) copy-start(f32[8]{0:T(128)} %param.16) | copy-start | bytes 100
  28.3 7.0 %collective-permute-start = (f32[8,128]{1,0:T(8,128)S(1)}, f32[8,128]{1,0:T(8,128)S(1)}, u32[]{:S(2)}, u32[]{:S(2)}) collective-permute-start(f32[8,128]{1,0:T(8,128)S(1)} %get-tuple-element.12), channel_id=1, source_target_pairs={{33,32},{32,33},{97,96},{96,97},{161,160},{160,161},{225,224},{224... | collective-permute-start | bytes 12296 | tf_op jit(solution)/shard_map/ppermute | solution.py:464

commit v5 on v4

--- a/solution.py
+++ b/solution.py
@@ -20,8 +20,10 @@
 NREG = 8
 CIRC = 16
 NSEC = SEC * CIRC
-RANK = 10
-ROWS = 48
+RANK = 9
+ROWS = 44
+QUAD = 4
+PADDED = 768
 EDGE = 4
 FIELD_ROWS = 40
 
@@ -48,12 +50,12 @@
     w = np.zeros((128, CIRC, ROWS))
     for a in range(2):
         for comp in range(COMP):
-            at = 20 * a + RANK * comp
+            at = RANK * (COMP * a + comp)
             w[32 * a + 16 * comp : 32 * a + 16 * comp + 16, :, at : at + RANK] = u
     for b in range(4):
-        first = 5 * (b % 2)
-        w[64 + 16 * b : 64 + 16 * b + 16, :, 40:45] = u[:, :, first : first + 5]
-    w = w.reshape(128, CIRC * ROWS)
+        part = u[:, :, 5 * (b % 2) : 5 * (b % 2) + 5]
+        w[64 + 16 * b : 64 + 16 * b + 16, :, 36 : 36 + part.shape[2]] = part
+    w = np.pad(w.reshape(128, CIRC * ROWS), ((0, 0), (0, PADDED - CIRC * ROWS)))
     hi = w.astype(ml_dtypes.bfloat16)
     lo = (w - hi.astype(np.float64)).astype(ml_dtypes.bfloat16)
     return np.concatenate([hi, lo])
@@ -92,9 +94,9 @@
     sub = row_of((8, SEC * COMP))
     parts = []
     for places in (
-        range(20),
-        range(4, 24),
-        [8 * b + i for b in range(4) for i in range(5)],
+        range(18),
+        range(2, 20),
+        [8 * b + (i + 4) % 8 for b in range(4) for i in range(5 - b % 2)],
     ):
         tiles = {}
         for place, row in zip(places, rows):
@@ -121,6 +123,7 @@
             )
             copies[u].start()
     rows = buf.reshape(LAY // 4, SEC * 4 * COMP, LANES)
+    send = send_ref.reshape(CIRC, ROWS, LANES)
     parity = lax.axis_index("sect") % 2
     tops = {}
     sums = {}
@@ -165,7 +168,7 @@
                 top = tops[32 + v]
                 if g:
                     top = pltpu.roll(top, LANES - 32 * g, 1)
-                tails[v, g] = jnp.where(sub == 7, top, y)
+                tails[v, g] = jnp.where(sub == 3, top, y)
 
     def pack(u):
         first = halves(sums[4 * u], sums[4 * u + 1])
@@ -174,11 +177,13 @@
         top1 = halves(tops[4 * u + 2], tops[4 * u + 3])
         for h in range(2):
             c = 2 * u + (h + parity) % 2
-            send_ref[c, 0:16] = first[h][0:16]
-            send_ref[c, 16:24] = first[h][16:24] + second[h][0:8]
-            send_ref[c, 24:40] = second[h][8:24]
-            tile = jnp.where(sub == 5, top0[h], tails[u // 2, quarter_of(u, h)])
-            send_ref[c, 40:48] = jnp.where(sub == 6, top1[h], tile)
+            tail = tails[u // 2, quarter_of(u, h)]
+            send[c, 0:16] = first[h][0:16]
+            send[c, 16:24] = first[h][16:24] + second[h][0:8]
+            send[c, 24:32] = second[h][8:16]
+            send[c, 32:40] = jnp.where(sub < 4, second[h][16:24], tail)
+            tile = jnp.where(sub == 1, top0[h], tail)
+            send[c, 40:44] = jnp.where(sub == 2, top1[h], tile)[0:4]
 
     a_ref[...] = window_matrix()
     waiting = []
@@ -200,7 +205,7 @@
         project_kernel,
         name="project",
         out_shape=[
-            jax.ShapeDtypeStruct((CIRC, ROWS, LANES), jnp.float32),
+            jax.ShapeDtypeStruct((CIRC, ROWS // QUAD, QUAD, LANES), jnp.float32),
             jax.ShapeDtypeStruct((LAY, SEC, LANES), jnp.float32),
         ],
         in_specs=[pl.BlockSpec(memory_space=pl.ANY)],
@@ -223,7 +228,8 @@
     is_left = h == 0
     lane = lane_of((1, LANES))
     sub = row_of((8, LANES))
-    p = recv_ref[...]
+    recv = recv_ref.reshape(CIRC * ROWS, LANES)
+    p = jnp.concatenate([recv[...], jnp.zeros((PADDED - CIRC * ROWS, LANES), jnp.float32)])
     hi = p.astype(jnp.bfloat16)
     lo = (p - hi.astype(jnp.float32)).astype(jnp.bfloat16)
     o = jnp.dot(
@@ -274,7 +280,7 @@
         share = jnp.zeros((1, LANES), jnp.float32)
         for r in range(NREG):
             share = jnp.where(region[i] == r, mullins_ref[0:1, r : r + 1], share)
-        top = jnp.max(recv_ref[pl.ds(45 + i, CIRC, stride=ROWS), :], axis=0, keepdims=True)
+        top = jnp.max(recv[pl.ds(41 + i, CIRC, stride=ROWS), :], axis=0, keepdims=True)
         peak = jnp.maximum(prior[i], top)
         heats.append(jnp.exp(-0.5 * temp[i]) * picked + share * (peak - prior[i]))
         peaks.append(peak)
@@ -454,7 +460,7 @@
     send, energy = project(strain.transpose(0, 2, 1, 3))
     recv = lax.all_to_all(send, "circ", 0, 0, tiled=True)
     own, msg = owner(
-        recv.reshape(CIRC * ROWS, LANES), w, region, prior, temp, cond, loss, mullins.reshape(1, NREG)
+        recv, w, region, prior, temp, cond, loss, mullins.reshape(1, NREG)
     )
     pairs = []
     for s in range(1, sects):

time: 52.1 us -> 51.4 us (0.987)
  blocking collectives: 38.9 us -> 38.2 us
    all_to_all x1, blocking collectives: 24.4 us -> 23.7 us  [per_device(): recv = lax.all_to_all(send, 'circ', 0, 0, tiled=True)]
where the time goes in v5:
time: 51.4 us; the launch traced here: 51.1 us
  blocking collectives  38.2 us (74%)
  waiting for transfers between devices  5.11 us (10%)
  Pallas kernels  5.09 us (10%)
  starting transfers between devices  1.91 us (4%)
  between operations  0.75 us (1%)
    all_to_all x1, blocking collectives, per_device(): recv = lax.all_to_all(send, 'circ', 0, 0, tiled=True)  23.7 us
    all_to_all x1, blocking collectives, per_device(): everything = lax.all_to_all(block, 'circ', 0, 0, tiled=True)  14.5 us
    ppermute x1, waiting for transfers between devices, per_device(): halo = lax.ppermute(msg, ('circ', 'sect'), pairs)  5.11 us
    pallas_call x1, Pallas kernels, project(): pl.pallas_call(project_kernel, name='project', out_shape=[jax.ShapeDtypeS...  2.65 us
    pallas_call x1, Pallas kernels, soften(): pl.pallas_call(modulus_kernel, name='modulus', out_shape=[jax.ShapeDtypeS...  1.92 us
    ppermute x1, starting transfers between devices, per_device(): halo = lax.ppermute(msg, ('circ', 'sect'), pairs)  1.91 us
  transfers between devices with their start and end apart: 1, of which 1 were waited for; matrix products, arithmetic and copies ran while one was open for 0% of the time, Pallas kernels for 0%

profile of v5, /device:TPU:256, one launch (start us, length us, event | category | flops | bytes accessed | tf_op | source)
XLA Modules:
  0.0 51.1 jit_solution(4613324961209137056)
XLA Ops:
  0.6 0.0 copy-start
  0.6 0.0 copy-start.3
  0.7 0.0 copy-start.2
  0.7 0.0 copy-start.1
  0.7 0.0 copy-start.6
  0.7 0.0 copy-start.5
  0.7 0.0 copy-start.4
  0.7 0.0 copy-start.7
  0.7 2.7 %project.1 = (f32[16,11,4,128]{3,2,1,0:T(4,128)S(1)}, f32[36,128,128]{2,1,0:T(8,128)S(1)}) custom-call(bf16[128,36,2,128]{3,2,1,0:T(2,128)(2,1)} %bitcast.8), custom_call_target="tpu_custom_call" | custom-call | tf_op jit(solution)/shard_map/project/pallas_call | solution.py:204
  3.4 23.7 %all_to_all.10.recv_ref = f32[16,11,4,128]{3,2,1,0:T(4,128)S(1)} all-to-all(f32[16,11,4,128]{3,2,1,0:T(4,128)S(1)} %get-tuple-element.10), channel_id=1, replica_groups=mesh['circ'=16,'sect'=32] {'circ'}, dimensions={0} | all-to-all | bytes 720896 | tf_op jit(solution)/shard_map/all_to_all | solution.py:461
  27.1 0.0 copy-done
  27.1 0.0 copy-done.3
  27.1 0.0 copy-done.2
  27.1 0.0 copy-done.1
  27.1 0.0 copy-done.6
  27.1 0.0 copy-done.5
  27.1 0.0 copy-done.4
  27.1 0.5 %owner.1 = (f32[8,128]{1,0:T(8,128)S(1)}, f32[8,128]{1,0:T(8,128)S(1)}) custom-call(f32[16,11,4,128]{3,2,1,0:T(4,128)S(1)} %all_to_all.10.recv_ref, bf16[256,768]{1,0:T(8,128)(2,1)S(1)} %copy-done, s32[36,128]{1,0:T(8,128)S(1)} %copy-done.1, f32[36,128]{1,0:T(8,128)S(1)} %copy-done.4, f32[36,128]{1,0:T(8,128)S(1)} %copy-done.2, f32[36,128]{1,0:T(8,128)S(1)} %copy-done.3, ...), custom_call_target="tpu_custom_call" | custom-call | tf_op jit(solution)/shard_map/owner/pallas_call | solution.py:319
  27.7 1.9 %collective-permute-start = (f32[8,128]{1,0:T(8,128)S(1)}, f32[8,128]{1,0:T(8,128)S(1)}, u32[]{:S(2)}, u32[]{:S(2)}) collective-permute-start(f32[8,128]{1,0:T(8,128)S(1)} %get-tuple-element.12), channel_id=1, source_target_pairs={{33,32},{32,33},{97,96},{96,97},{161,160},{160,161},{225,224},{224... | collective-permute-start | bytes 12296 | tf_op jit(solution)/shard_map/ppermute | solution.py:470
  29.6 5.1 %collective-permute-done = f32[8,128]{1,0:T(8,128)S(1)} collective-permute-done((f32[8,128]{1,0:T(8,128)S(1)}, f32[8,128]{1,0:T(8,128)S(1)}, u32[]{:S(2)}, u32[]{:S(2)}) %collective-permute-start) | collective-permute-done | bytes 4128 | tf_op jit(solution)/shard_map/ppermute | solution.py:470
  34.7 14.5 %all_to_all.11 = f32[16,8,128]{2,1,0:T(8,128)S(1)} all-to-all(f32[16,8,128]{2,1,0:T(8,128)S(1)} %broadcast_in_dim.2), channel_id=1, replica_groups=mesh['circ'=16,'sect'=32] {'circ'}, dimensions={0} | all-to-all | bytes 131072 | tf_op jit(solution)/shard_map/all_to_all | solution.py:472
  49.2 0.0 copy-done.7
  49.2 1.9 %modulus.1 = (f32[36,128]{1,0:T(8,128)}, f32[36,128]{1,0:T(8,128)}, bf16[36,128,128]{2,1,0:T(8,128)(2,1)}) custom-call(f32[128,128]{1,0:T(8,128)S(1)} %bitcast.5, f32[36,128,128]{2,1,0:T(8,128)S(1)} %get-tuple-element.13.energy_ref, s32[36,128]{1,0:T(8,128)S(1)} %copy-done.1, f32[36,128]{1,0:T(8,128)S(1)} %copy-done.2, f32[36,128]{1,0:T(8,128)S(1)} %copy-done.3, ...), custom_call_target="tpu_custom_call" | custom-call | tf_op jit(solution)/shard_map/modulus/pallas_call | solution.py:437
  (2 shorter events, 0.0 us)
Async XLA Ops:
  0.6 26.5 %copy-start = (bf16[256,768]{1,0:T(8,128)(2,1)S(1)}, bf16[256,768]{1,0:T(8,128)(2,1)}, u32[]{:S(2)}) copy-start(bf16[256,768]{1,0:T(8,128)(2,1)} %constant.2.clone.w_ref) | copy-start | bytes 1179652
  0.6 26.5 %copy-start.3 = (f32[36,128]{1,0:T(8,128)S(1)}, f32[36,128]{1,0:T(8,128)}, u32[]{:S(2)}) copy-start(f32[36,128]{1,0:T(8,128)} %cond_ref.3) | copy-start | bytes 55300
  0.7 26.4 %copy-start.2 = (f32[36,128]{1,0:T(8,128)S(1)}, f32[36,128]{1,0:T(8,128)}, u32[]{:S(2)}) copy-start(f32[36,128]{1,0:T(8,128)} %temp_ref.3) | copy-start | bytes 55300
  0.7 26.4 %copy-start.1 = (s32[36,128]{1,0:T(8,128)S(1)}, s32[36,128]{1,0:T(8,128)}, u32[]{:S(2)}) copy-start(s32[36,128]{1,0:T(8,128)} %region_ref.3) | copy-start | bytes 55300
  0.7 26.4 %copy-start.6 = (f32[8]{0:T(128)S(1)}, f32[8]{0:T(128)}, u32[]{:S(2)}) copy-start(f32[8]{0:T(128)} %param.15) | copy-start | bytes 100
  0.7 26.4 %copy-start.5 = (f32[8,8]{1,0:T(8,128)S(1)}, f32[8,8]{1,0:T(8,128)}, u32[]{:S(2)}) copy-start(f32[8,8]{1,0:T(8,128)} %loss_ref.1) | copy-start | bytes 772
  0.7 26.4 %copy-start.4 = (f32[36,128]{1,0:T(8,128)S(1)}, f32[36,128]{1,0:T(8,128)}, u32[]{:S(2)}) copy-start(f32[36,128]{1,0:T(8,128)} %prior_ref.1) | copy-start | bytes 55300
  0.7 48.5 %copy-start.7 = (f32[8]{0:T(128)S(1)}, f32[8]{0:T(128)}, u32[]{:S(2)}) copy-start(f32[8]{0:T(128)} %param.16) | copy-start | bytes 100
  27.7 7.0 %collective-permute-start = (f32[8,128]{1,0:T(8,128)S(1)}, f32[8,128]{1,0:T(8,128)S(1)}, u32[]{:S(2)}, u32[]{:S(2)}) collective-permute-start(f32[8,128]{1,0:T(8,128)S(1)} %get-tuple-element.12), channel_id=1, source_target_pairs={{33,32},{32,33},{97,96},{96,97},{161,160},{160,161},{225,224},{224... | collective-permute-start | bytes 12296 | tf_op jit(solution)/shard_map/ppermute | solution.py:470

commit v6 on v5

--- a/solution.py
+++ b/solution.py
@@ -77,6 +77,14 @@
     )
 
 
+def across(u):
+    return u if u < 4 else u + 8
+
+
+def within(u):
+    return u + 4
+
+
 def quarter_of(u, h):
     return 3 * h if u % 2 == 0 else 1 + h
 
@@ -111,7 +119,7 @@
 
 
 TAIL = 8
-ORDER = ((TAIL, 0, 1), (2, 3, 4), (5, 6, 7))
+ORDER = ((TAIL, 0), (1, 2, 3, 4), (5, 6, 7))
 
 
 def project_kernel(strain_hbm, send_ref, energy_ref, buf, a_ref, sem):
@@ -176,7 +184,7 @@
         top0 = halves(tops[4 * u], tops[4 * u + 1])
         top1 = halves(tops[4 * u + 2], tops[4 * u + 3])
         for h in range(2):
-            c = 2 * u + (h + parity) % 2
+            c = across(u) + (within(u) - across(u)) * ((h + parity) % 2)
             tail = tails[u // 2, quarter_of(u, h)]
             send[c, 0:16] = first[h][0:16]
             send[c, 16:24] = first[h][16:24] + second[h][0:8]
@@ -223,8 +231,8 @@
     recv_ref, w_ref, region_ref, prior_ref, temp_ref, cond_ref, loss_ref, mullins_ref, own_ref, msg_ref
 ):
     c = lax.axis_index("circ")
-    u = c // 2
-    h = (c + lax.axis_index("sect")) % 2
+    u = c % 4 + 4 * (c // 8)
+    h = (lax.axis_index("sect") + (c // 4 + 1) // 2) % 2
     is_left = h == 0
     lane = lane_of((1, LANES))
     sub = row_of((8, LANES))
@@ -337,8 +345,23 @@
 ):
     low = lane_of((8, LANES)) < 64
     lane = lane_of((FIELD_ROWS, LANES))
-    parity = lax.axis_index("sect") % 2
-    at = [8 * parity, 8 * (1 - parity)]
+    even = lax.axis_index("sect") % 2 == 0
+
+    def sides(k):
+        far = jnp.concatenate(
+            [all_ref[pl.ds(k, 4, stride=8), :], all_ref[pl.ds(96 + k, 4, stride=8), :]]
+        )
+        near = all_ref[pl.ds(32 + k, 8, stride=8), :]
+        return jnp.where(even, far, near), jnp.where(even, near, far)
+
+    def tail_sides(k, odd):
+        k = k + 8 * odd
+        far = jnp.concatenate(
+            [all_ref[pl.ds(k, 2, stride=16), :], all_ref[pl.ds(96 + k, 2, stride=16), :]]
+        )
+        near = all_ref[pl.ds(32 + k, 4, stride=16), :]
+        return jnp.where(even, far, near), jnp.where(even, near, far)
+
     for scratch in (heat_s, peak_s, halo_s, cond_s, temp_s):
         scratch[32:FIELD_ROWS] = jnp.zeros((8, LANES), jnp.float32)
     region_s[32:FIELD_ROWS] = jnp.zeros((8, LANES), jnp.int32)
@@ -347,15 +370,15 @@
     region_s[0:LAY] = region_ref[...]
     for a in range(2):
         for base, target in ((0, heat_s), (2, peak_s)):
-            left = all_ref[pl.ds(at[0] + base + a, 8, stride=16), :]
-            right = all_ref[pl.ds(at[1] + base + a, 8, stride=16), :]
+            left, right = sides(base + a)
             target[pl.ds(2 * a, 8, stride=4), :] = jnp.where(low, left, pltpu.roll(right, 64, 1))
             target[pl.ds(2 * a + 1, 8, stride=4), :] = jnp.where(low, pltpu.roll(left, 64, 1), right)
     small = lane_of((4, LANES))
     for base, target in ((4, heat_s), (5, peak_s)):
         row = jnp.zeros((4, LANES), jnp.float32)
+        parts = [tail_sides(base, odd) for odd in range(2)]
         for odd, h, g in ((0, 0, 0), (1, 0, 1), (1, 1, 2), (0, 1, 3)):
-            part = all_ref[pl.ds(at[h] + 16 * odd + base, 4, stride=32), :]
+            part = parts[odd][h]
             if g != 1:
                 part = pltpu.roll(part, (32 * g - 32) % LANES, 1)
             row = jnp.where(small // 32 == g, part, row)
@@ -363,10 +386,9 @@
     wide = lane_of((8, LANES))
     outer = (wide < 3 * EDGE) | (wide >= LANES - 3 * EDGE)
     for j in range(4):
-        both = all_ref[pl.ds(4 + j, 8, stride=16), :] + all_ref[pl.ds(12 + j, 8, stride=16), :]
-        halo_s[pl.ds(j, 8, stride=4), :] = jnp.where(outer, both, 0.0)
-    from_left = all_ref[pl.ds(at[0] + 6, 4, stride=32), :]
-    from_right = all_ref[pl.ds(at[1] + 6, 4, stride=32), :]
+        left, right = sides(4 + j)
+        halo_s[pl.ds(j, 8, stride=4), :] = jnp.where(outer, left + right, 0.0)
+    from_left, from_right = tail_sides(6, 0)
     from_left = pltpu.roll(from_left, 32, 1)
     from_right = pltpu.roll(from_right, 96, 1)
     halo_s[32:LAY] = jnp.where(
@@ -464,8 +486,8 @@
     )
     pairs = []
     for s in range(1, sects):
-        for c in range(s % 2, CIRC, 2):
-            here = c * sects + s
+        for u in range(CIRC // 2):
+            here = (within(u) if s % 2 else across(u)) * sects + s
             pairs += [(here, here - 1), (here - 1, here)]
     halo = lax.ppermute(msg, ("circ", "sect"), pairs)
     block = jnp.broadcast_to((own + halo)[None], (CIRC, 8, LANES))

time: 51.4 us -> 50.3 us (0.979)
  blocking collectives: 38.2 us -> 37.3 us
    all_to_all x1, blocking collectives: 14.5 us -> 13.5 us  [per_device(): everything = lax.all_to_all(block, 'circ', 0, 0, tiled=True)]
where the time goes in v6:
time: 50.3 us; the launch traced here: 50.1 us
  blocking collectives  37.3 us (74%)
  waiting for transfers between devices  5.11 us (10%)
  Pallas kernels  4.98 us (10%)
  starting transfers between devices  1.91 us (4%)
  between operations  0.75 us (1%)
    all_to_all x1, blocking collectives, per_device(): recv = lax.all_to_all(send, 'circ', 0, 0, tiled=True)  23.7 us
    all_to_all x1, blocking collectives, per_device(): everything = lax.all_to_all(block, 'circ', 0, 0, tiled=True)  13.5 us
    ppermute x1, waiting for transfers between devices, per_device(): halo = lax.ppermute(msg, ('circ', 'sect'), pairs)  5.11 us
    pallas_call x1, Pallas kernels, project(): pl.pallas_call(project_kernel, name='project', out_shape=[jax.ShapeDtypeS...  2.56 us
    ppermute x1, starting transfers between devices, per_device(): halo = lax.ppermute(msg, ('circ', 'sect'), pairs)  1.91 us
    pallas_call x1, Pallas kernels, soften(): pl.pallas_call(modulus_kernel, name='modulus', out_shape=[jax.ShapeDtypeS...  1.9 us
  transfers between devices with their start and end apart: 1, of which 1 were waited for; matrix products, arithmetic and copies ran while one was open for 0% of the time, Pallas kernels for 0%

profile of v6, /device:TPU:256, one launch (start us, length us, event | category | flops | bytes accessed | tf_op | source)
XLA Modules:
  0.0 50.1 jit_solution(15327999202214995765)
XLA Ops:
  0.6 0.0 copy-start
  0.6 0.0 copy-start.3
  0.7 0.0 copy-start.2
  0.7 0.0 copy-start.1
  0.7 0.0 copy-start.6
  0.7 0.0 copy-start.5
  0.7 0.0 copy-start.4
  0.7 0.0 copy-start.7
  0.7 2.6 %project.1 = (f32[16,11,4,128]{3,2,1,0:T(4,128)S(1)}, f32[36,128,128]{2,1,0:T(8,128)S(1)}) custom-call(bf16[128,36,2,128]{3,2,1,0:T(2,128)(2,1)} %bitcast.8), custom_call_target="tpu_custom_call" | custom-call | tf_op jit(solution)/shard_map/project/pallas_call | solution.py:212
  3.3 23.7 %all_to_all.10.recv_ref = f32[16,11,4,128]{3,2,1,0:T(4,128)S(1)} all-to-all(f32[16,11,4,128]{3,2,1,0:T(4,128)S(1)} %get-tuple-element.10), channel_id=1, replica_groups=mesh['circ'=16,'sect'=32] {'circ'}, dimensions={0} | all-to-all | bytes 720896 | tf_op jit(solution)/shard_map/all_to_all | solution.py:483
  27.0 0.0 copy-done
  27.0 0.0 copy-done.3
  27.0 0.0 copy-done.2
  27.0 0.0 copy-done.1
  27.0 0.0 copy-done.6
  27.0 0.0 copy-done.5
  27.1 0.0 copy-done.4
  27.1 0.5 %owner.1 = (f32[8,128]{1,0:T(8,128)S(1)}, f32[8,128]{1,0:T(8,128)S(1)}) custom-call(f32[16,11,4,128]{3,2,1,0:T(4,128)S(1)} %all_to_all.10.recv_ref, bf16[256,768]{1,0:T(8,128)(2,1)S(1)} %copy-done, s32[36,128]{1,0:T(8,128)S(1)} %copy-done.1, f32[36,128]{1,0:T(8,128)S(1)} %copy-done.4, f32[36,128]{1,0:T(8,128)S(1)} %copy-done.2, f32[36,128]{1,0:T(8,128)S(1)} %copy-done.3, ...), custom_call_target="tpu_custom_call" | custom-call | tf_op jit(solution)/shard_map/owner/pallas_call | solution.py:327
  27.6 1.9 %collective-permute-start = (f32[8,128]{1,0:T(8,128)S(1)}, f32[8,128]{1,0:T(8,128)S(1)}, u32[]{:S(2)}, u32[]{:S(2)}) collective-permute-start(f32[8,128]{1,0:T(8,128)S(1)} %get-tuple-element.12), channel_id=1, source_target_pairs={{129,128},{128,129},{161,160},{160,161},{193,192},{192,193},{225,2... | collective-permute-start | bytes 12296 | tf_op jit(solution)/shard_map/ppermute | solution.py:492
  29.5 5.1 %collective-permute-done = f32[8,128]{1,0:T(8,128)S(1)} collective-permute-done((f32[8,128]{1,0:T(8,128)S(1)}, f32[8,128]{1,0:T(8,128)S(1)}, u32[]{:S(2)}, u32[]{:S(2)}) %collective-permute-start) | collective-permute-done | bytes 4128 | tf_op jit(solution)/shard_map/ppermute | solution.py:492
  34.6 13.5 %all_to_all.11 = f32[16,8,128]{2,1,0:T(8,128)S(1)} all-to-all(f32[16,8,128]{2,1,0:T(8,128)S(1)} %broadcast_in_dim.2), channel_id=1, replica_groups=mesh['circ'=16,'sect'=32] {'circ'}, dimensions={0} | all-to-all | bytes 131072 | tf_op jit(solution)/shard_map/all_to_all | solution.py:494
  48.2 0.0 copy-done.7
  48.2 1.9 %modulus.1 = (f32[36,128]{1,0:T(8,128)}, f32[36,128]{1,0:T(8,128)}, bf16[36,128,128]{2,1,0:T(8,128)(2,1)}) custom-call(f32[128,128]{1,0:T(8,128)S(1)} %bitcast.5, f32[36,128,128]{2,1,0:T(8,128)S(1)} %get-tuple-element.13.energy_ref, s32[36,128]{1,0:T(8,128)S(1)} %copy-done.1, f32[36,128]{1,0:T(8,128)S(1)} %copy-done.2, f32[36,128]{1,0:T(8,128)S(1)} %copy-done.3, ...), custom_call_target="tpu_custom_call" | custom-call | tf_op jit(solution)/shard_map/modulus/pallas_call | solution.py:459
  (2 shorter events, 0.0 us)
Async XLA Ops:
  0.6 26.4 %copy-start = (bf16[256,768]{1,0:T(8,128)(2,1)S(1)}, bf16[256,768]{1,0:T(8,128)(2,1)}, u32[]{:S(2)}) copy-start(bf16[256,768]{1,0:T(8,128)(2,1)} %constant.2.clone.w_ref) | copy-start | bytes 1179652
  0.6 26.4 %copy-start.3 = (f32[36,128]{1,0:T(8,128)S(1)}, f32[36,128]{1,0:T(8,128)}, u32[]{:S(2)}) copy-start(f32[36,128]{1,0:T(8,128)} %cond_ref.3) | copy-start | bytes 55300
  0.7 26.4 %copy-start.2 = (f32[36,128]{1,0:T(8,128)S(1)}, f32[36,128]{1,0:T(8,128)}, u32[]{:S(2)}) copy-start(f32[36,128]{1,0:T(8,128)} %temp_ref.3) | copy-start | bytes 55300
  0.7 26.4 %copy-start.1 = (s32[36,128]{1,0:T(8,128)S(1)}, s32[36,128]{1,0:T(8,128)}, u32[]{:S(2)}) copy-start(s32[36,128]{1,0:T(8,128)} %region_ref.3) | copy-start | bytes 55300
  0.7 26.4 %copy-start.6 = (f32[8]{0:T(128)S(1)}, f32[8]{0:T(128)}, u32[]{:S(2)}) copy-start(f32[8]{0:T(128)} %param.15) | copy-start | bytes 100
  0.7 26.4 %copy-start.5 = (f32[8,8]{1,0:T(8,128)S(1)}, f32[8,8]{1,0:T(8,128)}, u32[]{:S(2)}) copy-start(f32[8,8]{1,0:T(8,128)} %loss_ref.1) | copy-start | bytes 772
  0.7 26.4 %copy-start.4 = (f32[36,128]{1,0:T(8,128)S(1)}, f32[36,128]{1,0:T(8,128)}, u32[]{:S(2)}) copy-start(f32[36,128]{1,0:T(8,128)} %prior_ref.1) | copy-start | bytes 55300
  0.7 47.5 %copy-start.7 = (f32[8]{0:T(128)S(1)}, f32[8]{0:T(128)}, u32[]{:S(2)}) copy-start(f32[8]{0:T(128)} %param.16) | copy-start | bytes 100
  27.6 7.0 %collective-permute-start = (f32[8,128]{1,0:T(8,128)S(1)}, f32[8,128]{1,0:T(8,128)S(1)}, u32[]{:S(2)}, u32[]{:S(2)}) collective-permute-start(f32[8,128]{1,0:T(8,128)S(1)} %get-tuple-element.12), channel_id=1, source_target_pairs={{129,128},{128,129},{161,160},{160,161},{193,192},{192,193},{225,2... | collective-permute-start | bytes 12296 | tf_op jit(solution)/shard_map/ppermute | solution.py:492

commit v7 on v6

--- a/solution.py
+++ b/solution.py
@@ -261,37 +261,48 @@
     quarter = jnp.where(u % 2 == 0, 3 * h, 1 + h)
     back = (LANES - 32 * quarter) % LANES
 
-    def natural(ref):
-        rows = [ref[pl.ds(4 * u + j, 1), :] for j in range(4)]
-        rows.append(ref[pl.ds(32 + u // 2, 1), :])
-        return rows
-
-    def packed(rows):
-        out = []
-        for a in range(2):
-            left, right = halves(rows[2 * a], rows[2 * a + 1])
-            out.append(jnp.where(is_left, left, right))
-        out.append(pltpu.roll(rows[4], back, 1))
-        return out
-
-    region = packed(natural(region_ref))
-    prior = packed(natural(prior_ref))
-    temp_rows = natural(temp_ref)
-    temp = packed(temp_rows)
-    cond_rows = natural(cond_ref)
-    heats, peaks = [], []
+    low = lane_of((4, LANES)) < 64
+
+    def stacked(vectors):
+        out = jnp.where(sub == 0, vectors[0], vectors[1])
+        return jnp.where(sub == 2, vectors[2], out)
+
+    def own_cells(ref):
+        rows = ref[pl.ds(4 * u, 4), :]
+        last = ref[pl.ds(32 + u // 2, 1), :]
+        turned = pltpu.roll(rows, 64, 1)
+        evens = jnp.where(is_left, rows, turned)
+        odds = jnp.where(is_left, turned, rows)
+        odds = pltpu.roll(jnp.concatenate([odds, odds]), 7, 0)[0:4]
+        mixed = jnp.where(low, evens, odds)
+        return stacked([mixed[0:1], mixed[2:3], pltpu.roll(last, back, 1)]), rows, last
+
+    region, _, _ = own_cells(region_ref)
+    prior, _, _ = own_cells(prior_ref)
+    temp, temp_rows, temp_last = own_cells(temp_ref)
+    cond_rows = cond_ref[pl.ds(4 * u, 4), :]
+    cond_last = cond_ref[pl.ds(32 + u // 2, 1), :]
+    picked = []
     for i in range(3):
         q = loss_ref[:, 0:1] * powers[i][0:1]
         for k in range(1, HARM):
             q = q + loss_ref[:, k : k + 1] * powers[i][k : k + 1]
-        picked = jnp.sum(jnp.where(region[i] == sub, q, 0.0), axis=0, keepdims=True)
-        share = jnp.zeros((1, LANES), jnp.float32)
-        for r in range(NREG):
-            share = jnp.where(region[i] == r, mullins_ref[0:1, r : r + 1], share)
-        top = jnp.max(recv[pl.ds(41 + i, CIRC, stride=ROWS), :], axis=0, keepdims=True)
-        peak = jnp.maximum(prior[i], top)
-        heats.append(jnp.exp(-0.5 * temp[i]) * picked + share * (peak - prior[i]))
-        peaks.append(peak)
+        picked.append(
+            jnp.sum(jnp.where(region[i : i + 1] == sub, q, 0.0), axis=0, keepdims=True)
+        )
+    share = jnp.zeros((8, LANES), jnp.float32)
+    for r in range(NREG):
+        share = jnp.where(region == r, mullins_ref[0:1, r : r + 1], share)
+    top = stacked(
+        [
+            jnp.max(recv[pl.ds(41 + i, CIRC, stride=ROWS), :], axis=0, keepdims=True)
+            for i in range(3)
+        ]
+    )
+    peak = jnp.maximum(prior, top)
+    heat = jnp.exp(-0.5 * temp) * stacked(picked) + share * (peak - prior)
+    heats = [heat[i : i + 1] for i in range(3)]
+    peaks = [peak[i : i + 1] for i in range(3)]
 
     third = (lane >= 32) & (lane < 64)
     own = jnp.where(sub == 0, heats[0], 0.0)
@@ -301,24 +312,23 @@
     own = jnp.where((sub == 4) & third, pltpu.roll(heats[2], 32, 1), own)
     own_ref[...] = jnp.where((sub == 5) & third, pltpu.roll(peaks[2], 32, 1), own)
 
-    edge_heat = []
-    for a in range(2):
-        turned = pltpu.roll(heats[a], 64, 1)
-        edge_heat.append(jnp.where(is_left, heats[a], turned))
-        edge_heat.append(jnp.where(is_left, turned, heats[a]))
-    edge_heat.append(jnp.where(is_left, heats[2], pltpu.roll(heats[2], 96, 1)))
     edge = jnp.where(is_left, lane, LANES - 1 - lane) < EDGE
     step = jnp.where(is_left, EDGE, LANES - EDGE)
-    msg = jnp.zeros((8, LANES), jnp.float32)
-    for j in range(5):
-        row = jnp.where(edge, edge_heat[j], 0.0)
-        row = row + pltpu.roll(jnp.where(edge, cond_rows[j], 0.0), step, 1)
-        row = row + pltpu.roll(jnp.where(edge, temp_rows[j], 0.0), (2 * step) % LANES, 1)
-        if j < 4:
-            msg = msg + jnp.where(sub == 4 + j, row, 0.0)
-        else:
-            row = pltpu.roll(row, jnp.where(is_left, 32, 96), 1)
-            msg = msg + jnp.where(sub == 6, row, 0.0)
+
+    def message(heat_rows, cond_part, temp_part):
+        row = jnp.where(edge, heat_rows, 0.0)
+        row = row + pltpu.roll(jnp.where(edge, cond_part, 0.0), step, 1)
+        return row + pltpu.roll(jnp.where(edge, temp_part, 0.0), (2 * step) % LANES, 1)
+
+    turned = pltpu.roll(heat, 64, 1)
+    evens = jnp.where(is_left, heat, turned)
+    odds = jnp.where(is_left, turned, heat)
+    four = jnp.concatenate([evens[0:1], odds[0:1], evens[1:2], odds[1:2]])
+    main = message(four, cond_rows, temp_rows)
+    final = jnp.where(is_left, heats[2], pltpu.roll(heats[2], 96, 1))
+    final = pltpu.roll(message(final, cond_last, temp_last), jnp.where(is_left, 32, 96), 1)
+    msg = jnp.concatenate([jnp.zeros((4, LANES), jnp.float32), main])
+    msg = msg + jnp.where(sub == 6, final, 0.0)
     msg_ref[...] = msg
 
 

time: 50.3 us -> 50.3 us (level)
  no operation moved by 1% of the time
where the time goes in v7:
time: 50.3 us; the launch traced here: 50.1 us
  blocking collectives  37.3 us (74%)
  waiting for transfers between devices  5.11 us (10%)
  Pallas kernels  4.98 us (10%)
  starting transfers between devices  1.92 us (4%)
  between operations  0.75 us (1%)
    all_to_all x1, blocking collectives, per_device(): recv = lax.all_to_all(send, 'circ', 0, 0, tiled=True)  23.7 us
    all_to_all x1, blocking collectives, per_device(): everything = lax.all_to_all(block, 'circ', 0, 0, tiled=True)  13.5 us
    ppermute x1, waiting for transfers between devices, per_device(): halo = lax.ppermute(msg, ('circ', 'sect'), pairs)  5.11 us
    pallas_call x1, Pallas kernels, project(): pl.pallas_call(project_kernel, name='project', out_shape=[jax.ShapeDtypeS...  2.56 us
    ppermute x1, starting transfers between devices, per_device(): halo = lax.ppermute(msg, ('circ', 'sect'), pairs)  1.92 us
    pallas_call x1, Pallas kernels, soften(): pl.pallas_call(modulus_kernel, name='modulus', out_shape=[jax.ShapeDtypeS...  1.9 us
  transfers between devices with their start and end apart: 1, of which 1 were waited for; matrix products, arithmetic and copies ran while one was open for 0% of the time, Pallas kernels for 0%

profile of v7, /device:TPU:256, one launch (start us, length us, event | category | flops | bytes accessed | tf_op | source)
XLA Modules:
  0.0 50.1 jit_solution(15566273345091987640)
XLA Ops:
  0.6 0.0 copy-start
  0.6 0.0 copy-start.3
  0.7 0.0 copy-start.2
  0.7 0.0 copy-start.1
  0.7 0.0 copy-start.6
  0.7 0.0 copy-start.5
  0.7 0.0 copy-start.4
  0.7 0.0 copy-start.7
  0.7 2.6 %project.1 = (f32[16,11,4,128]{3,2,1,0:T(4,128)S(1)}, f32[36,128,128]{2,1,0:T(8,128)S(1)}) custom-call(bf16[128,36,2,128]{3,2,1,0:T(2,128)(2,1)} %bitcast.8), custom_call_target="tpu_custom_call" | custom-call | tf_op jit(solution)/shard_map/project/pallas_call | solution.py:212
  3.3 23.7 %all_to_all.10.recv_ref = f32[16,11,4,128]{3,2,1,0:T(4,128)S(1)} all-to-all(f32[16,11,4,128]{3,2,1,0:T(4,128)S(1)} %get-tuple-element.10), channel_id=1, replica_groups=mesh['circ'=16,'sect'=32] {'circ'}, dimensions={0} | all-to-all | bytes 720896 | tf_op jit(solution)/shard_map/all_to_all | solution.py:493
  27.0 0.0 copy-done
  27.0 0.0 copy-done.3
  27.0 0.0 copy-done.2
  27.0 0.0 copy-done.1
  27.0 0.0 copy-done.6
  27.0 0.0 copy-done.5
  27.1 0.0 copy-done.4
  27.1 0.5 %owner.1 = (f32[8,128]{1,0:T(8,128)S(1)}, f32[8,128]{1,0:T(8,128)S(1)}) custom-call(f32[16,11,4,128]{3,2,1,0:T(4,128)S(1)} %all_to_all.10.recv_ref, bf16[256,768]{1,0:T(8,128)(2,1)S(1)} %copy-done, s32[36,128]{1,0:T(8,128)S(1)} %copy-done.1, f32[36,128]{1,0:T(8,128)S(1)} %copy-done.4, f32[36,128]{1,0:T(8,128)S(1)} %copy-done.2, f32[36,128]{1,0:T(8,128)S(1)} %copy-done.3, ...), custom_call_target="tpu_custom_call" | custom-call | tf_op jit(solution)/shard_map/owner/pallas_call | solution.py:337
  27.6 1.9 %collective-permute-start = (f32[8,128]{1,0:T(8,128)S(1)}, f32[8,128]{1,0:T(8,128)S(1)}, u32[]{:S(2)}, u32[]{:S(2)}) collective-permute-start(f32[8,128]{1,0:T(8,128)S(1)} %get-tuple-element.12), channel_id=1, source_target_pairs={{129,128},{128,129},{161,160},{160,161},{193,192},{192,193},{225,2... | collective-permute-start | bytes 12296 | tf_op jit(solution)/shard_map/ppermute | solution.py:502
  29.5 5.1 %collective-permute-done = f32[8,128]{1,0:T(8,128)S(1)} collective-permute-done((f32[8,128]{1,0:T(8,128)S(1)}, f32[8,128]{1,0:T(8,128)S(1)}, u32[]{:S(2)}, u32[]{:S(2)}) %collective-permute-start) | collective-permute-done | bytes 4128 | tf_op jit(solution)/shard_map/ppermute | solution.py:502
  34.6 13.5 %all_to_all.11 = f32[16,8,128]{2,1,0:T(8,128)S(1)} all-to-all(f32[16,8,128]{2,1,0:T(8,128)S(1)} %broadcast_in_dim.2), channel_id=1, replica_groups=mesh['circ'=16,'sect'=32] {'circ'}, dimensions={0} | all-to-all | bytes 131072 | tf_op jit(solution)/shard_map/all_to_all | solution.py:504
  48.2 0.0 copy-done.7
  48.2 1.9 %modulus.1 = (f32[36,128]{1,0:T(8,128)}, f32[36,128]{1,0:T(8,128)}, bf16[36,128,128]{2,1,0:T(8,128)(2,1)}) custom-call(f32[128,128]{1,0:T(8,128)S(1)} %bitcast.5, f32[36,128,128]{2,1,0:T(8,128)S(1)} %get-tuple-element.13.energy_ref, s32[36,128]{1,0:T(8,128)S(1)} %copy-done.1, f32[36,128]{1,0:T(8,128)S(1)} %copy-done.2, f32[36,128]{1,0:T(8,128)S(1)} %copy-done.3, ...), custom_call_target="tpu_custom_call" | custom-call | tf_op jit(solution)/shard_map/modulus/pallas_call | solution.py:469
  (2 shorter events, 0.0 us)
Async XLA Ops:
  0.6 26.4 %copy-start = (bf16[256,768]{1,0:T(8,128)(2,1)S(1)}, bf16[256,768]{1,0:T(8,128)(2,1)}, u32[]{:S(2)}) copy-start(bf16[256,768]{1,0:T(8,128)(2,1)} %constant.2.clone.w_ref) | copy-start | bytes 1179652
  0.6 26.4 %copy-start.3 = (f32[36,128]{1,0:T(8,128)S(1)}, f32[36,128]{1,0:T(8,128)}, u32[]{:S(2)}) copy-start(f32[36,128]{1,0:T(8,128)} %cond_ref.3) | copy-start | bytes 55300
  0.7 26.4 %copy-start.2 = (f32[36,128]{1,0:T(8,128)S(1)}, f32[36,128]{1,0:T(8,128)}, u32[]{:S(2)}) copy-start(f32[36,128]{1,0:T(8,128)} %temp_ref.3) | copy-start | bytes 55300
  0.7 26.4 %copy-start.1 = (s32[36,128]{1,0:T(8,128)S(1)}, s32[36,128]{1,0:T(8,128)}, u32[]{:S(2)}) copy-start(s32[36,128]{1,0:T(8,128)} %region_ref.3) | copy-start | bytes 55300
  0.7 26.4 %copy-start.6 = (f32[8]{0:T(128)S(1)}, f32[8]{0:T(128)}, u32[]{:S(2)}) copy-start(f32[8]{0:T(128)} %param.15) | copy-start | bytes 100
  0.7 26.4 %copy-start.5 = (f32[8,8]{1,0:T(8,128)S(1)}, f32[8,8]{1,0:T(8,128)}, u32[]{:S(2)}) copy-start(f32[8,8]{1,0:T(8,128)} %loss_ref.1) | copy-start | bytes 772
  0.7 26.4 %copy-start.4 = (f32[36,128]{1,0:T(8,128)S(1)}, f32[36,128]{1,0:T(8,128)}, u32[]{:S(2)}) copy-start(f32[36,128]{1,0:T(8,128)} %prior_ref.1) | copy-start | bytes 55300
  0.7 47.5 %copy-start.7 = (f32[8]{0:T(128)S(1)}, f32[8]{0:T(128)}, u32[]{:S(2)}) copy-start(f32[8]{0:T(128)} %param.16) | copy-start | bytes 100
  27.6 7.0 %collective-permute-start = (f32[8,128]{1,0:T(8,128)S(1)}, f32[8,128]{1,0:T(8,128)S(1)}, u32[]{:S(2)}, u32[]{:S(2)}) collective-permute-start(f32[8,128]{1,0:T(8,128)S(1)} %get-tuple-element.12), channel_id=1, source_target_pairs={{129,128},{128,129},{161,160},{160,161},{193,192},{192,193},{225,2... | collective-permute-start | bytes 12296 | tf_op jit(solution)/shard_map/ppermute | solution.py:502

commit v8 on v7

--- a/solution.py
+++ b/solution.py
@@ -129,7 +129,7 @@
             copies[u] = pltpu.make_async_copy(
                 strain_hbm.at[:, pl.ds(4 * u, 4)], buf.at[u], sem.at[u]
             )
-            copies[u].start()
+            copies[u].start(priority=1)
     rows = buf.reshape(LAY // 4, SEC * 4 * COMP, LANES)
     send = send_ref.reshape(CIRC, ROWS, LANES)
     parity = lax.axis_index("sect") % 2

time: 50.3 us -> 50.3 us (level)
  no operation moved by 1% of the time
where the time goes in v8:
time: 50.3 us; the launch traced here: 50.1 us
  blocking collectives  37.3 us (74%)
  waiting for transfers between devices  5.11 us (10%)
  Pallas kernels  4.98 us (10%)
  starting transfers between devices  1.92 us (4%)
  between operations  0.75 us (1%)
    all_to_all x1, blocking collectives, per_device(): recv = lax.all_to_all(send, 'circ', 0, 0, tiled=True)  23.7 us
    all_to_all x1, blocking collectives, per_device(): everything = lax.all_to_all(block, 'circ', 0, 0, tiled=True)  13.5 us
    ppermute x1, waiting for transfers between devices, per_device(): halo = lax.ppermute(msg, ('circ', 'sect'), pairs)  5.11 us
    pallas_call x1, Pallas kernels, project(): pl.pallas_call(project_kernel, name='project', out_shape=[jax.ShapeDtypeS...  2.56 us
    ppermute x1, starting transfers between devices, per_device(): halo = lax.ppermute(msg, ('circ', 'sect'), pairs)  1.92 us
    pallas_call x1, Pallas kernels, soften(): pl.pallas_call(modulus_kernel, name='modulus', out_shape=[jax.ShapeDtypeS...  1.9 us
  transfers between devices with their start and end apart: 1, of which 1 were waited for; matrix products, arithmetic and copies ran while one was open for 0% of the time, Pallas kernels for 0%

profile of v8, /device:TPU:256, one launch (start us, length us, event | category | flops | bytes accessed | tf_op | source)
XLA Modules:
  0.0 50.1 jit_solution(18379312480200930764)
XLA Ops:
  0.6 0.0 copy-start
  0.6 0.0 copy-start.3
  0.7 0.0 copy-start.2
  0.7 0.0 copy-start.1
  0.7 0.0 copy-start.6
  0.7 0.0 copy-start.5
  0.7 0.0 copy-start.4
  0.7 0.0 copy-start.7
  0.7 2.6 %project.1 = (f32[16,11,4,128]{3,2,1,0:T(4,128)S(1)}, f32[36,128,128]{2,1,0:T(8,128)S(1)}) custom-call(bf16[128,36,2,128]{3,2,1,0:T(2,128)(2,1)} %bitcast.8), custom_call_target="tpu_custom_call" | custom-call | tf_op jit(solution)/shard_map/project/pallas_call | solution.py:212
  3.3 23.7 %all_to_all.10.recv_ref = f32[16,11,4,128]{3,2,1,0:T(4,128)S(1)} all-to-all(f32[16,11,4,128]{3,2,1,0:T(4,128)S(1)} %get-tuple-element.10), channel_id=1, replica_groups=mesh['circ'=16,'sect'=32] {'circ'}, dimensions={0} | all-to-all | bytes 720896 | tf_op jit(solution)/shard_map/all_to_all | solution.py:493
  27.0 0.0 copy-done
  27.0 0.0 copy-done.3
  27.0 0.0 copy-done.2
  27.0 0.0 copy-done.1
  27.0 0.0 copy-done.6
  27.0 0.0 copy-done.5
  27.1 0.0 copy-done.4
  27.1 0.5 %owner.1 = (f32[8,128]{1,0:T(8,128)S(1)}, f32[8,128]{1,0:T(8,128)S(1)}) custom-call(f32[16,11,4,128]{3,2,1,0:T(4,128)S(1)} %all_to_all.10.recv_ref, bf16[256,768]{1,0:T(8,128)(2,1)S(1)} %copy-done, s32[36,128]{1,0:T(8,128)S(1)} %copy-done.1, f32[36,128]{1,0:T(8,128)S(1)} %copy-done.4, f32[36,128]{1,0:T(8,128)S(1)} %copy-done.2, f32[36,128]{1,0:T(8,128)S(1)} %copy-done.3, ...), custom_call_target="tpu_custom_call" | custom-call | tf_op jit(solution)/shard_map/owner/pallas_call | solution.py:337
  27.6 1.9 %collective-permute-start = (f32[8,128]{1,0:T(8,128)S(1)}, f32[8,128]{1,0:T(8,128)S(1)}, u32[]{:S(2)}, u32[]{:S(2)}) collective-permute-start(f32[8,128]{1,0:T(8,128)S(1)} %get-tuple-element.12), channel_id=1, source_target_pairs={{129,128},{128,129},{161,160},{160,161},{193,192},{192,193},{225,2... | collective-permute-start | bytes 12296 | tf_op jit(solution)/shard_map/ppermute | solution.py:502
  29.5 5.1 %collective-permute-done = f32[8,128]{1,0:T(8,128)S(1)} collective-permute-done((f32[8,128]{1,0:T(8,128)S(1)}, f32[8,128]{1,0:T(8,128)S(1)}, u32[]{:S(2)}, u32[]{:S(2)}) %collective-permute-start) | collective-permute-done | bytes 4128 | tf_op jit(solution)/shard_map/ppermute | solution.py:502
  34.6 13.5 %all_to_all.11 = f32[16,8,128]{2,1,0:T(8,128)S(1)} all-to-all(f32[16,8,128]{2,1,0:T(8,128)S(1)} %broadcast_in_dim.2), channel_id=1, replica_groups=mesh['circ'=16,'sect'=32] {'circ'}, dimensions={0} | all-to-all | bytes 131072 | tf_op jit(solution)/shard_map/all_to_all | solution.py:504
  48.2 0.0 copy-done.7
  48.2 1.9 %modulus.1 = (f32[36,128]{1,0:T(8,128)}, f32[36,128]{1,0:T(8,128)}, bf16[36,128,128]{2,1,0:T(8,128)(2,1)}) custom-call(f32[128,128]{1,0:T(8,128)S(1)} %bitcast.5, f32[36,128,128]{2,1,0:T(8,128)S(1)} %get-tuple-element.13.energy_ref, s32[36,128]{1,0:T(8,128)S(1)} %copy-done.1, f32[36,128]{1,0:T(8,128)S(1)} %copy-done.2, f32[36,128]{1,0:T(8,128)S(1)} %copy-done.3, ...), custom_call_target="tpu_custom_call" | custom-call | tf_op jit(solution)/shard_map/modulus/pallas_call | solution.py:469
  (2 shorter events, 0.0 us)
Async XLA Ops:
  0.6 26.4 %copy-start = (bf16[256,768]{1,0:T(8,128)(2,1)S(1)}, bf16[256,768]{1,0:T(8,128)(2,1)}, u32[]{:S(2)}) copy-start(bf16[256,768]{1,0:T(8,128)(2,1)} %constant.2.clone.w_ref) | copy-start | bytes 1179652
  0.6 26.4 %copy-start.3 = (f32[36,128]{1,0:T(8,128)S(1)}, f32[36,128]{1,0:T(8,128)}, u32[]{:S(2)}) copy-start(f32[36,128]{1,0:T(8,128)} %cond_ref.3) | copy-start | bytes 55300
  0.7 26.4 %copy-start.2 = (f32[36,128]{1,0:T(8,128)S(1)}, f32[36,128]{1,0:T(8,128)}, u32[]{:S(2)}) copy-start(f32[36,128]{1,0:T(8,128)} %temp_ref.3) | copy-start | bytes 55300
  0.7 26.4 %copy-start.1 = (s32[36,128]{1,0:T(8,128)S(1)}, s32[36,128]{1,0:T(8,128)}, u32[]{:S(2)}) copy-start(s32[36,128]{1,0:T(8,128)} %region_ref.3) | copy-start | bytes 55300
  0.7 26.4 %copy-start.6 = (f32[8]{0:T(128)S(1)}, f32[8]{0:T(128)}, u32[]{:S(2)}) copy-start(f32[8]{0:T(128)} %param.15) | copy-start | bytes 100
  0.7 26.4 %copy-start.5 = (f32[8,8]{1,0:T(8,128)S(1)}, f32[8,8]{1,0:T(8,128)}, u32[]{:S(2)}) copy-start(f32[8,8]{1,0:T(8,128)} %loss_ref.1) | copy-start | bytes 772
  0.7 26.4 %copy-start.4 = (f32[36,128]{1,0:T(8,128)S(1)}, f32[36,128]{1,0:T(8,128)}, u32[]{:S(2)}) copy-start(f32[36,128]{1,0:T(8,128)} %prior_ref.1) | copy-start | bytes 55300
  0.7 47.5 %copy-start.7 = (f32[8]{0:T(128)S(1)}, f32[8]{0:T(128)}, u32[]{:S(2)}) copy-start(f32[8]{0:T(128)} %param.16) | copy-start | bytes 100
  27.6 7.0 %collective-permute-start = (f32[8,128]{1,0:T(8,128)S(1)}, f32[8,128]{1,0:T(8,128)S(1)}, u32[]{:S(2)}, u32[]{:S(2)}) collective-permute-start(f32[8,128]{1,0:T(8,128)S(1)} %get-tuple-element.12), channel_id=1, source_target_pairs={{129,128},{128,129},{161,160},{160,161},{193,192},{192,193},{225,2... | collective-permute-start | bytes 12296 | tf_op jit(solution)/shard_map/ppermute | solution.py:502

commit v9 on v7

--- a/solution.py
+++ b/solution.py
@@ -345,7 +345,7 @@
 
 
 GROUPS = 6
-EARLY = 12
+EARLY = 24
 
 
 def modulus_kernel(

time: 50.3 us -> 50.3 us (level)
  no operation moved by 1% of the time
where the time goes in v9:
time: 50.3 us; the launch traced here: 50.1 us
  blocking collectives  37.3 us (74%)
  waiting for transfers between devices  5.11 us (10%)
  Pallas kernels  4.98 us (10%)
  starting transfers between devices  1.92 us (4%)
  between operations  0.75 us (1%)
    all_to_all x1, blocking collectives, per_device(): recv = lax.all_to_all(send, 'circ', 0, 0, tiled=True)  23.7 us
    all_to_all x1, blocking collectives, per_device(): everything = lax.all_to_all(block, 'circ', 0, 0, tiled=True)  13.5 us
    ppermute x1, waiting for transfers between devices, per_device(): halo = lax.ppermute(msg, ('circ', 'sect'), pairs)  5.11 us
    pallas_call x1, Pallas kernels, project(): pl.pallas_call(project_kernel, name='project', out_shape=[jax.ShapeDtypeS...  2.56 us
    ppermute x1, starting transfers between devices, per_device(): halo = lax.ppermute(msg, ('circ', 'sect'), pairs)  1.92 us
    pallas_call x1, Pallas kernels, soften(): pl.pallas_call(modulus_kernel, name='modulus', out_shape=[jax.ShapeDtypeS...  1.9 us
  transfers between devices with their start and end apart: 1, of which 1 were waited for; matrix products, arithmetic and copies ran while one was open for 0% of the time, Pallas kernels for 0%

profile of v9, /device:TPU:256, one launch (start us, length us, event | category | flops | bytes accessed | tf_op | source)
XLA Modules:
  0.0 50.1 jit_solution(9471625672241503053)
XLA Ops:
  0.6 0.0 copy-start
  0.6 0.0 copy-start.3
  0.7 0.0 copy-start.2
  0.7 0.0 copy-start.1
  0.7 0.0 copy-start.6
  0.7 0.0 copy-start.5
  0.7 0.0 copy-start.4
  0.7 0.0 copy-start.7
  0.7 2.6 %project.1 = (f32[16,11,4,128]{3,2,1,0:T(4,128)S(1)}, f32[36,128,128]{2,1,0:T(8,128)S(1)}) custom-call(bf16[128,36,2,128]{3,2,1,0:T(2,128)(2,1)} %bitcast.8), custom_call_target="tpu_custom_call" | custom-call | tf_op jit(solution)/shard_map/project/pallas_call | solution.py:212
  3.3 23.7 %all_to_all.10.recv_ref = f32[16,11,4,128]{3,2,1,0:T(4,128)S(1)} all-to-all(f32[16,11,4,128]{3,2,1,0:T(4,128)S(1)} %get-tuple-element.10), channel_id=1, replica_groups=mesh['circ'=16,'sect'=32] {'circ'}, dimensions={0} | all-to-all | bytes 720896 | tf_op jit(solution)/shard_map/all_to_all | solution.py:493
  27.0 0.0 copy-done
  27.0 0.0 copy-done.3
  27.0 0.0 copy-done.2
  27.0 0.0 copy-done.1
  27.0 0.0 copy-done.6
  27.0 0.0 copy-done.5
  27.1 0.0 copy-done.4
  27.1 0.5 %owner.1 = (f32[8,128]{1,0:T(8,128)S(1)}, f32[8,128]{1,0:T(8,128)S(1)}) custom-call(f32[16,11,4,128]{3,2,1,0:T(4,128)S(1)} %all_to_all.10.recv_ref, bf16[256,768]{1,0:T(8,128)(2,1)S(1)} %copy-done, s32[36,128]{1,0:T(8,128)S(1)} %copy-done.1, f32[36,128]{1,0:T(8,128)S(1)} %copy-done.4, f32[36,128]{1,0:T(8,128)S(1)} %copy-done.2, f32[36,128]{1,0:T(8,128)S(1)} %copy-done.3, ...), custom_call_target="tpu_custom_call" | custom-call | tf_op jit(solution)/shard_map/owner/pallas_call | solution.py:337
  27.6 1.9 %collective-permute-start = (f32[8,128]{1,0:T(8,128)S(1)}, f32[8,128]{1,0:T(8,128)S(1)}, u32[]{:S(2)}, u32[]{:S(2)}) collective-permute-start(f32[8,128]{1,0:T(8,128)S(1)} %get-tuple-element.12), channel_id=1, source_target_pairs={{129,128},{128,129},{161,160},{160,161},{193,192},{192,193},{225,2... | collective-permute-start | bytes 12296 | tf_op jit(solution)/shard_map/ppermute | solution.py:502
  29.5 5.1 %collective-permute-done = f32[8,128]{1,0:T(8,128)S(1)} collective-permute-done((f32[8,128]{1,0:T(8,128)S(1)}, f32[8,128]{1,0:T(8,128)S(1)}, u32[]{:S(2)}, u32[]{:S(2)}) %collective-permute-start) | collective-permute-done | bytes 4128 | tf_op jit(solution)/shard_map/ppermute | solution.py:502
  34.6 13.5 %all_to_all.11 = f32[16,8,128]{2,1,0:T(8,128)S(1)} all-to-all(f32[16,8,128]{2,1,0:T(8,128)S(1)} %broadcast_in_dim.2), channel_id=1, replica_groups=mesh['circ'=16,'sect'=32] {'circ'}, dimensions={0} | all-to-all | bytes 131072 | tf_op jit(solution)/shard_map/all_to_all | solution.py:504
  48.2 0.0 copy-done.7
  48.2 1.9 %modulus.1 = (f32[36,128]{1,0:T(8,128)}, f32[36,128]{1,0:T(8,128)}, bf16[36,128,128]{2,1,0:T(8,128)(2,1)}) custom-call(f32[128,128]{1,0:T(8,128)S(1)} %bitcast.5, f32[36,128,128]{2,1,0:T(8,128)S(1)} %get-tuple-element.13.energy_ref, s32[36,128]{1,0:T(8,128)S(1)} %copy-done.1, f32[36,128]{1,0:T(8,128)S(1)} %copy-done.2, f32[36,128]{1,0:T(8,128)S(1)} %copy-done.3, ...), custom_call_target="tpu_custom_call" | custom-call | tf_op jit(solution)/shard_map/modulus/pallas_call | solution.py:469
  (2 shorter events, 0.0 us)
Async XLA Ops:
  0.6 26.4 %copy-start = (bf16[256,768]{1,0:T(8,128)(2,1)S(1)}, bf16[256,768]{1,0:T(8,128)(2,1)}, u32[]{:S(2)}) copy-start(bf16[256,768]{1,0:T(8,128)(2,1)} %constant.2.clone.w_ref) | copy-start | bytes 1179652
  0.6 26.4 %copy-start.3 = (f32[36,128]{1,0:T(8,128)S(1)}, f32[36,128]{1,0:T(8,128)}, u32[]{:S(2)}) copy-start(f32[36,128]{1,0:T(8,128)} %cond_ref.3) | copy-start | bytes 55300
  0.7 26.4 %copy-start.2 = (f32[36,128]{1,0:T(8,128)S(1)}, f32[36,128]{1,0:T(8,128)}, u32[]{:S(2)}) copy-start(f32[36,128]{1,0:T(8,128)} %temp_ref.3) | copy-start | bytes 55300
  0.7 26.4 %copy-start.1 = (s32[36,128]{1,0:T(8,128)S(1)}, s32[36,128]{1,0:T(8,128)}, u32[]{:S(2)}) copy-start(s32[36,128]{1,0:T(8,128)} %region_ref.3) | copy-start | bytes 55300
  0.7 26.4 %copy-start.6 = (f32[8]{0:T(128)S(1)}, f32[8]{0:T(128)}, u32[]{:S(2)}) copy-start(f32[8]{0:T(128)} %param.15) | copy-start | bytes 100
  0.7 26.4 %copy-start.5 = (f32[8,8]{1,0:T(8,128)S(1)}, f32[8,8]{1,0:T(8,128)}, u32[]{:S(2)}) copy-start(f32[8,8]{1,0:T(8,128)} %loss_ref.1) | copy-start | bytes 772
  0.7 26.4 %copy-start.4 = (f32[36,128]{1,0:T(8,128)S(1)}, f32[36,128]{1,0:T(8,128)}, u32[]{:S(2)}) copy-start(f32[36,128]{1,0:T(8,128)} %prior_ref.1) | copy-start | bytes 55300
  0.7 47.5 %copy-start.7 = (f32[8]{0:T(128)S(1)}, f32[8]{0:T(128)}, u32[]{:S(2)}) copy-start(f32[8]{0:T(128)} %param.16) | copy-start | bytes 100
  27.6 7.0 %collective-permute-start = (f32[8,128]{1,0:T(8,128)S(1)}, f32[8,128]{1,0:T(8,128)S(1)}, u32[]{:S(2)}, u32[]{:S(2)}) collective-permute-start(f32[8,128]{1,0:T(8,128)S(1)} %get-tuple-element.12), channel_id=1, source_target_pairs={{129,128},{128,129},{161,160},{160,161},{193,192},{192,193},{225,2... | collective-permute-start | bytes 12296 | tf_op jit(solution)/shard_map/ppermute | solution.py:502
